TPU v7x, 256 devices: a whole 4x4x8 slice. The times are simulated.
256 devices in a mesh: section: 8 (over z_lo, core), dp: 32 (over z_hi, x, y).
Axes of the slice: x: 4, y: 4, z: 8 (z_hi: 2, z_lo: 4; z = z_hi * 4 + z_lo), core: 2. Of those that a mesh axis runs over, the one named last changes fastest.
Arguments:
- acts: bfloat16 [16, 2, 32, 128, 4096], P('section', None, 'dp'), may hold values from -6 to 6
- gates: bfloat16 [16, 2, 32, 128, 4096], P('section', None, 'dp'), may hold values from -6 to 6
- filters: bfloat16 [16, 256, 128], P('section', 'dp'), may hold values from -0.15625 to 0.15625
- bases: bfloat16 [16, 4096, 128], P('section', 'dp'), may hold values from -0.09375 to 0.09375
- final_hidden: bfloat16 [2, 32, 128, 4096], P(None, 'dp'), may hold values from -40 to 40
- unembed: bfloat16 [4096, 512], P('dp'), may hold values from -0.09375 to 0.09375
- targets: int32 [2, 32, 128], P(None, 'dp'), may hold values from 0 to 511
Outputs:
- features: float32 [2, 32, 4096], P(None, 'dp')
All inputs are finite; a program needn't handle non-finite values.
Results may differ from a plain program's by a relative error of at most 0.02.
Values may be sent and summed in bfloat16 or wider, within the bound.
No kernel may reach another device: no remote copies, remote signals or barrier semaphores. Data moves between devices by JAX's collectives and lax.ppermute only.
A program may use at most 128 MiB of HBM per device.

v0:
```python
import jax
import jax.numpy as jnp
from jax import lax
from jax.sharding import PartitionSpec as P


def shifted(value, axis, steps):
    count = lax.axis_size(axis)
    leading, last = (max(0, -steps), min(count, count - steps))
    return lax.ppermute(value, axis, [(source, source + steps) for source in range(leading, last)])


def band_pair(kernel):
    taps = kernel.shape[1]
    offset = jnp.arange(taps)[None, :] - jnp.arange(taps)[:, None]
    within = jnp.where(offset[None] >= 0, kernel[:, jnp.clip(offset, 0, taps - 1)], 0.0)
    across = jnp.where(offset[None] < 0, kernel[:, jnp.clip(offset + taps, 0, taps - 1)], 0.0)
    return (within, across)


def spread_back(values, within):
    seq_len = values.shape[0]
    model_dim = values.shape[1]
    groups = within.shape[0]
    taps = within.shape[1]
    blocks = values.reshape(seq_len // taps, taps, groups, model_dim // groups)
    summed = jnp.einsum("gtu,bugc->btgc", within, blocks, preferred_element_type=jnp.float32)
    return summed.reshape(seq_len, model_dim)


def shards(acts, gates, filters, bases, final_hidden, unembed, targets):
    kernels, basis_all = (
        lax.all_gather(filters, "dp", axis=1, tiled=True),
        lax.all_gather(bases, "dp", axis=1, tiled=True),
    )
    sections = lax.axis_size("section")
    section_idx = lax.axis_index("section")
    layers_here = acts.shape[0]
    micro_count = acts.shape[1]
    seq_len = acts.shape[3]
    model_dim = acts.shape[4]
    proj_rank = bases.shape[2] // 2
    vocab_size = unembed.shape[1]
    hidden_rows = final_hidden.reshape(micro_count * seq_len, model_dim)
    target_rows = targets.reshape(micro_count * seq_len)
    contract_last = (((1,), (1,)), ((), ()))
    vocab_full = lax.all_gather(unembed, "dp", axis=0, tiled=True)
    logits = jnp.dot(hidden_rows, vocab_full, preferred_element_type=jnp.float32)
    row_peak = jnp.max(logits, axis=1, keepdims=True)
    exp_terms = jnp.exp(logits - row_peak)
    probabilities = exp_terms / jnp.sum(exp_terms, axis=1, keepdims=True)
    onehot = (target_rows[:, None] == jnp.arange(vocab_size)[None, :]).astype(jnp.float32)
    dlogits = (probabilities - onehot).astype(jnp.bfloat16)
    top_flat = lax.dot_general(
        dlogits, vocab_full, contract_last, preferred_element_type=jnp.float32
    )
    top_flat = top_flat.astype(jnp.bfloat16)
    top_cot = top_flat.reshape(micro_count, seq_len, model_dim)
    empty_term = jnp.zeros((1, proj_rank * proj_rank), jnp.float32)
    band_pairs = [band_pair(kernels[layer_no]) for layer_no in range(layers_here)]

    def layer_work(operands):
        cotangent, micro_slot = operands
        feature_term = empty_term
        for layer_no in reversed(range(layers_here)):
            saved_act = lax.dynamic_index_in_dim(acts[layer_no], micro_slot, 0, keepdims=False)[0]
            gate_now = lax.dynamic_index_in_dim(gates[layer_no], micro_slot, 0, keepdims=False)[0]
            rows_in = jnp.dot(
                saved_act, basis_all[layer_no, :, :proj_rank], preferred_element_type=jnp.float32
            )
            rows_out = jnp.dot(
                cotangent, basis_all[layer_no, :, proj_rank:], preferred_element_type=jnp.float32
            )
            outer_sum = jnp.einsum("to,ti->oi", rows_out, rows_in, precision=lax.Precision.HIGHEST)
            feature_term = feature_term + outer_sum.reshape(1, proj_rank * proj_rank)
            scaled = (gate_now.astype(jnp.float32) * cotangent.astype(jnp.float32)).astype(
                jnp.bfloat16
            )
            within, across = band_pairs[layer_no]
            cotangent = (cotangent.astype(jnp.float32) + spread_back(scaled, within)).astype(
                jnp.bfloat16
            )
        return (cotangent, feature_term)

    def skip_work(operands):
        return (operands[0], empty_term)

    def tick(tick_step, carry):
        incoming, feats = carry
        micro_slot = tick_step - (sections - 1 - section_idx)
        is_live = (micro_slot >= 0) & (micro_slot < micro_count)
        slot_clip = jnp.clip(micro_slot, 0, micro_count - 1)
        top_now = lax.dynamic_index_in_dim(top_cot, slot_clip, 0, keepdims=False)
        cotangent = jnp.where(section_idx == sections - 1, top_now, incoming)
        cotangent, feature_term = lax.cond(is_live, layer_work, skip_work, (cotangent, slot_clip))
        chosen = (jnp.arange(micro_count) == slot_clip) & is_live
        feats = feats + jnp.where(chosen[:, None, None], feature_term[None], 0.0)
        passed = shifted(cotangent, "section", -1)
        return (passed, feats)

    start = (
        jnp.zeros((seq_len, model_dim), jnp.bfloat16),
        jnp.zeros((micro_count, 1, proj_rank * proj_rank), jnp.float32),
    )
    final_pair = lax.fori_loop(0, micro_count + sections - 1, tick, start)
    feats_done = final_pair[1]
    return lax.psum(feats_done, "section")


def solution(mesh):
    in_specs = (
        P("section", None, "dp", None, None),
        P("section", None, "dp", None, None),
        P("section", "dp", None),
        P("section", "dp", None),
        P(None, "dp", None, None),
        P("dp", None),
        P(None, "dp", None),
    )
    out_specs = P(None, "dp", None)
    return jax.shard_map(shards, mesh=mesh, in_specs=in_specs, out_specs=out_specs, check_vma=False)
```

profile of v0, /device:TPU:0, one launch (start us, length us, event | category | flops | bytes accessed | tf_op | source)
XLA Modules:
  0.0 635.8 jit_solution(10929711650794690809)
XLA Ops:
  8.7 120.7 %all_gather.10 = bf16[2,256,128]{2,0,1:T(2,128)(2,1)S(1)} all-gather(bf16[2,8,128]{2,0,1:T(2,128)(2,1)S(1)} %copy.18), channel_id=1, replica_groups=mesh['section'=8,'dp'=32] {'dp'}, dimensions={1}, use_global_device_ids=true | all-gather | bytes 135168 | tf_op jit(solution)/shard_map/all_gather | solution.py:33
  129.8 65.2 %gather_fusion = bf16[16384,256]{1,0:T(8,128)(2,1)} fusion(bf16[256,128]{0,1:T(8,128)(2,1)S(1)} %bitcast.75, s32[16384]{0:T(1024)S(1)} %fusion.28), kind=kCustom, calls=%fused_computation | custom fusion | bytes 16842752 | tf_op jit(solution)/shard_map/gather | solution.py:16
  195.0 12.4 %copy.20 = bf16[128,128,256]{1,0,2:T(8,128)(2,1)} copy(bf16[128,128,256]{2,1,0:T(8,128)(2,1)} %bitcast.80) | data formatting | bytes 16777216 | tf_op jit(solution)/shard_map/gather | solution.py:16
  207.6 65.2 %gather_fusion.1 = bf16[16384,256]{1,0:T(8,128)(2,1)} fusion(bf16[256,128]{0,1:T(8,128)(2,1)S(1)} %bitcast.76, s32[16384]{0:T(1024)S(1)} %fusion.28), kind=kCustom, calls=%fused_computation.1 | custom fusion | bytes 16842752 | tf_op jit(solution)/shard_map/gather | solution.py:16
  272.8 12.4 %copy.22 = bf16[128,128,256]{1,0,2:T(8,128)(2,1)} copy(bf16[128,128,256]{2,1,0:T(8,128)(2,1)} %bitcast.79) | data formatting | bytes 16777216 | tf_op jit(solution)/shard_map/gather | solution.py:16
  285.2 6.3 copy.24
  291.5 11.5 %select_bitcast_fusion = (bf16[256,128,128]{2,1,0:T(8,128)(2,1)}, bf16[256,128,128]{2,1,0:T(8,128)(2,1)}) fusion(bf16[128,128,256]{1,0,2:T(8,128)(2,1)} %copy.22, pred[128,128]{1,0:T(8,128)(4,1)S(1)} %subtract_compare_fusion, bf16[128,128,256]{1,0,2:T(8,128)(2,1)} %copy.20), kind=kLoop, calls=%fused_computation.35 | loop fusion | flops 8388608 | bytes 33570816 | tf_op jit(solution)/shard_map/jit(_where)/select_n | solution.py:16
  303.1 3.7 fusion.33
  307.0 2.7 convolution_convert_fusion
  309.9 291.0 %while.18 = (s32[]{:T(128)}, bf16[128,4096]{0,1:T(8,128)(2,1)S(1)}, f32[2,1,4096]{2,1,0:T(1,128)S(1)}, s32[]{:T(128)}, pred[]{:T(512)}, /*index=5*/bf16[2,128,40...) while((s32[]{:T(128)}, bf16[128,4096]{0,1:T(8,128)(2,1)S(1)}, ...), condition=%wide.region_5.6_spmd.clone, body=%wide.region_2.5_spmd.clone.sunk | while | flops 557346816 | bytes 132547016 | solution.py:105
  310.1 1.3 constant_dynamic-slice_fusion.2
  312.2 1.3 collective-permute-start
  313.7 3.1 collective-permute-done
  316.8 1.3 constant_dynamic-slice_fusion.2
  319.0 1.3 collective-permute-start
  320.4 13.5 %collective-permute-done = bf16[128,4096]{0,1:T(8,128)(2,1)S(1)} collective-permute-done((bf16[128,4096]{0,1:T(8,128)(2,1)S(1)}, bf16[128,4096]{0,1:T(8,128)(2,1)S(1)}, u32[]{:S(2)}, u32[]{:S(2)}) %collective-permute-start) | collective-permute-done | bytes 1048608 | tf_op jit(solution)/shard_map/while/body/eval_jaxpr/ppermute | solution.py:10
  333.9 1.3 constant_dynamic-slice_fusion.2
  336.0 1.3 collective-permute-start
  337.4 14.7 %collective-permute-done = bf16[128,4096]{0,1:T(8,128)(2,1)S(1)} collective-permute-done((bf16[128,4096]{0,1:T(8,128)(2,1)S(1)}, bf16[128,4096]{0,1:T(8,128)(2,1)S(1)}, u32[]{:S(2)}, u32[]{:S(2)}) %collective-permute-start) | collective-permute-done | bytes 1048608 | tf_op jit(solution)/shard_map/while/body/eval_jaxpr/ppermute | solution.py:10
  352.1 1.3 constant_dynamic-slice_fusion.2
  354.3 1.3 collective-permute-start
  355.7 14.7 %collective-permute-done = bf16[128,4096]{0,1:T(8,128)(2,1)S(1)} collective-permute-done((bf16[128,4096]{0,1:T(8,128)(2,1)S(1)}, bf16[128,4096]{0,1:T(8,128)(2,1)S(1)}, u32[]{:S(2)}, u32[]{:S(2)}) %collective-permute-start) | collective-permute-done | bytes 1048608 | tf_op jit(solution)/shard_map/while/body/eval_jaxpr/ppermute | solution.py:10
  370.4 1.3 constant_dynamic-slice_fusion.2
  372.6 1.3 collective-permute-start
  374.0 14.7 %collective-permute-done = bf16[128,4096]{0,1:T(8,128)(2,1)S(1)} collective-permute-done((bf16[128,4096]{0,1:T(8,128)(2,1)S(1)}, bf16[128,4096]{0,1:T(8,128)(2,1)S(1)}, u32[]{:S(2)}, u32[]{:S(2)}) %collective-permute-start) | collective-permute-done | bytes 1048608 | tf_op jit(solution)/shard_map/while/body/eval_jaxpr/ppermute | solution.py:10
  388.7 1.3 constant_dynamic-slice_fusion.2
  390.9 1.3 collective-permute-start
  392.3 14.7 %collective-permute-done = bf16[128,4096]{0,1:T(8,128)(2,1)S(1)} collective-permute-done((bf16[128,4096]{0,1:T(8,128)(2,1)S(1)}, bf16[128,4096]{0,1:T(8,128)(2,1)S(1)}, u32[]{:S(2)}, u32[]{:S(2)}) %collective-permute-start) | collective-permute-done | bytes 1048608 | tf_op jit(solution)/shard_map/while/body/eval_jaxpr/ppermute | solution.py:10
  407.0 1.3 constant_dynamic-slice_fusion.2
  409.1 1.3 collective-permute-start
  410.6 121.2 %collective-permute-done = bf16[128,4096]{0,1:T(8,128)(2,1)S(1)} collective-permute-done((bf16[128,4096]{0,1:T(8,128)(2,1)S(1)}, bf16[128,4096]{0,1:T(8,128)(2,1)S(1)}, u32[]{:S(2)}, u32[]{:S(2)}) %collective-permute-start) | collective-permute-done | bytes 1048608 | tf_op jit(solution)/shard_map/while/body/eval_jaxpr/ppermute | solution.py:10
  531.7 1.3 constant_dynamic-slice_fusion.2
  533.9 22.1 %conditional.3 = (bf16[128,4096]{0,1:T(8,128)(2,1)S(1)}, f32[1,4096]{1,0:T(1,128)S(1)}) conditional(s32[]{:T(128)} %convert_element_type.83, bf16[128,4096]{0,1:T(8,128)(2,1)S(1)} %bitcast_select_fusion.2, (bf16[128,4096]{0,1:T(8,128)(2,1)S(1)}, bf16[2,2,1,128,4096]{3,4,2,1,0:T(8,128)(2,1)}, s32[]{:T(128)}, bf16[256,128,128]{2,1,0:T(8,128)(2,1)}, ...), branch_computations={%region_3.3_spmd, %region_4.4_spmd} | conditional | flops 556797952 | bytes 120930448 | solution.py:95
  533.9 2.6 fusion.31
  536.8 1.7 copy-done.2
  538.5 4.5 fusion.34
  549.0 6.8 %fusion.35 = f32[256,16,128]{2,1,0:T(8,128)S(1)} fusion(bf16[128,256,16]{0,2,1:T(8,128)(2,1)S(1)} %bitcast.77, bf16[256,128,128]{2,1,0:T(8,128)(2,1)} %get-tuple-element.249), kind=kOutput, calls=%fused_computation.54 | convolution fusion | flops 134217728 | bytes 11534336 | tf_op jit(solution)/shard_map/while/body/eval_jaxpr/cond/branch_1_fun/gtu,bugc->btgc/dot_general | solution.py:27
  556.0 1.3 collective-permute-start
  557.4 14.7 %collective-permute-done = bf16[128,4096]{0,1:T(8,128)(2,1)S(1)} collective-permute-done((bf16[128,4096]{0,1:T(8,128)(2,1)S(1)}, bf16[128,4096]{0,1:T(8,128)(2,1)S(1)}, u32[]{:S(2)}, u32[]{:S(2)}) %collective-permute-start) | collective-permute-done | bytes 1048608 | tf_op jit(solution)/shard_map/while/body/eval_jaxpr/ppermute | solution.py:10
  572.1 1.3 constant_dynamic-slice_fusion.2
  574.2 22.1 %conditional.3 = (bf16[128,4096]{0,1:T(8,128)(2,1)S(1)}, f32[1,4096]{1,0:T(1,128)S(1)}) conditional(s32[]{:T(128)} %convert_element_type.83, bf16[128,4096]{0,1:T(8,128)(2,1)S(1)} %bitcast_select_fusion.2, (bf16[128,4096]{0,1:T(8,128)(2,1)S(1)}, bf16[2,2,1,128,4096]{3,4,2,1,0:T(8,128)(2,1)}, s32[]{:T(128)}, bf16[256,128,128]{2,1,0:T(8,128)(2,1)}, ...), branch_computations={%region_3.3_spmd, %region_4.4_spmd} | conditional | flops 556797952 | bytes 120930448 | solution.py:95
  574.2 2.6 fusion.31
  577.2 1.7 copy-done.2
  578.9 4.5 fusion.34
  589.3 6.8 %fusion.35 = f32[256,16,128]{2,1,0:T(8,128)S(1)} fusion(bf16[128,256,16]{0,2,1:T(8,128)(2,1)S(1)} %bitcast.77, bf16[256,128,128]{2,1,0:T(8,128)(2,1)} %get-tuple-element.249), kind=kOutput, calls=%fused_computation.54 | convolution fusion | flops 134217728 | bytes 11534336 | tf_op jit(solution)/shard_map/while/body/eval_jaxpr/cond/branch_1_fun/gtu,bugc->btgc/dot_general | solution.py:27
  596.3 1.3 collective-permute-start
  597.7 3.1 collective-permute-done
  600.9 28.1 %psum.7 = f32[2,1,4096]{2,1,0:T(1,128)} all-reduce(f32[2,1,4096]{2,1,0:T(1,128)S(1)} %get-tuple-element.267), channel_id=1, replica_groups=mesh['section'=8,'dp'=32] {'section'}, use_global_device_ids=true, to_apply=%region_6.7 | all-reduce | flops 8192 | bytes 65536 | tf_op jit(solution)/shard_map/psum | solution.py:107
  (105 shorter events, 24.2 us)
Async XLA Ops:
  6.5 296.6 %copy-start = (bf16[2,1,128,4096]{3,2,1,0:T(8,128)(2,1)S(1)}, bf16[2,1,128,4096]{3,2,1,0:T(8,128)(2,1)}, u32[]{:S(2)}) copy-start(bf16[2,1,128,4096]{3,2,1,0:T(8,128)(2,1)} %param.15) | copy-start | bytes 6291460
  6.5 296.5 %all-gather.3.cloned.1.call-start = ((), (), s32[]{:S(2)}) async-start(), calls=%async_computation | async-start | bytes 4325376 | tf_op jit(solution)/shard_map/all_gather | solution.py:47
  7.3 302.5 %all-gather.5.cloned.1.call-start = ((), (), s32[]{:S(2)}) async-start(), calls=%async_computation.1 | async-start | bytes 2162688 | tf_op jit(solution)/shard_map/all_gather | solution.py:34
  303.1 3.9 copy-start.5
  303.1 3.9 copy-start.6
  312.2 4.6 collective-permute-start
  319.0 14.9 %collective-permute-start = (bf16[128,4096]{0,1:T(8,128)(2,1)S(1)}, bf16[128,4096]{0,1:T(8,128)(2,1)S(1)}, u32[]{:S(2)}, u32[]{:S(2)}) collective-permute-start(bf16[128,4096]{0,1:T(8,128)(2,1)S(1)} %get-tuple-element.442), channel_id=1, source_target_pairs={{32,0},{64,32},{96,64},{128,96},{160,128},{192,160},{224,192},{33,... | collective-permute-start | bytes 3145736 | tf_op jit(solution)/shard_map/while/body/eval_jaxpr/ppermute | solution.py:10
  336.0 16.1 %collective-permute-start = (bf16[128,4096]{0,1:T(8,128)(2,1)S(1)}, bf16[128,4096]{0,1:T(8,128)(2,1)S(1)}, u32[]{:S(2)}, u32[]{:S(2)}) collective-permute-start(bf16[128,4096]{0,1:T(8,128)(2,1)S(1)} %get-tuple-element.442), channel_id=1, source_target_pairs={{32,0},{64,32},{96,64},{128,96},{160,128},{192,160},{224,192},{33,... | collective-permute-start | bytes 3145736 | tf_op jit(solution)/shard_map/while/body/eval_jaxpr/ppermute | solution.py:10
  354.3 16.1 %collective-permute-start = (bf16[128,4096]{0,1:T(8,128)(2,1)S(1)}, bf16[128,4096]{0,1:T(8,128)(2,1)S(1)}, u32[]{:S(2)}, u32[]{:S(2)}) collective-permute-start(bf16[128,4096]{0,1:T(8,128)(2,1)S(1)} %get-tuple-element.442), channel_id=1, source_target_pairs={{32,0},{64,32},{96,64},{128,96},{160,128},{192,160},{224,192},{33,... | collective-permute-start | bytes 3145736 | tf_op jit(solution)/shard_map/while/body/eval_jaxpr/ppermute | solution.py:10
  372.6 16.1 %collective-permute-start = (bf16[128,4096]{0,1:T(8,128)(2,1)S(1)}, bf16[128,4096]{0,1:T(8,128)(2,1)S(1)}, u32[]{:S(2)}, u32[]{:S(2)}) collective-permute-start(bf16[128,4096]{0,1:T(8,128)(2,1)S(1)} %get-tuple-element.442), channel_id=1, source_target_pairs={{32,0},{64,32},{96,64},{128,96},{160,128},{192,160},{224,192},{33,... | collective-permute-start | bytes 3145736 | tf_op jit(solution)/shard_map/while/body/eval_jaxpr/ppermute | solution.py:10
  390.9 16.1 %collective-permute-start = (bf16[128,4096]{0,1:T(8,128)(2,1)S(1)}, bf16[128,4096]{0,1:T(8,128)(2,1)S(1)}, u32[]{:S(2)}, u32[]{:S(2)}) collective-permute-start(bf16[128,4096]{0,1:T(8,128)(2,1)S(1)} %get-tuple-element.442), channel_id=1, source_target_pairs={{32,0},{64,32},{96,64},{128,96},{160,128},{192,160},{224,192},{33,... | collective-permute-start | bytes 3145736 | tf_op jit(solution)/shard_map/while/body/eval_jaxpr/ppermute | solution.py:10
  409.1 122.6 %collective-permute-start = (bf16[128,4096]{0,1:T(8,128)(2,1)S(1)}, bf16[128,4096]{0,1:T(8,128)(2,1)S(1)}, u32[]{:S(2)}, u32[]{:S(2)}) collective-permute-start(bf16[128,4096]{0,1:T(8,128)(2,1)S(1)} %get-tuple-element.442), channel_id=1, source_target_pairs={{32,0},{64,32},{96,64},{128,96},{160,128},{192,160},{224,192},{33,... | collective-permute-start | bytes 3145736 | tf_op jit(solution)/shard_map/while/body/eval_jaxpr/ppermute | solution.py:10
  533.9 4.6 copy-start.2
  543.0 1.6 copy-start.4
  543.0 2.8 copy-start.3
  556.0 16.1 %collective-permute-start = (bf16[128,4096]{0,1:T(8,128)(2,1)S(1)}, bf16[128,4096]{0,1:T(8,128)(2,1)S(1)}, u32[]{:S(2)}, u32[]{:S(2)}) collective-permute-start(bf16[128,4096]{0,1:T(8,128)(2,1)S(1)} %get-tuple-element.442), channel_id=1, source_target_pairs={{32,0},{64,32},{96,64},{128,96},{160,128},{192,160},{224,192},{33,... | collective-permute-start | bytes 3145736 | tf_op jit(solution)/shard_map/while/body/eval_jaxpr/ppermute | solution.py:10
  574.2 4.6 copy-start.2
  583.3 1.6 copy-start.4
  583.3 2.8 copy-start.3
  596.3 4.6 collective-permute-start
  600.8 28.1 %copy-start.1 = (bf16[2,1,128,4096]{3,2,1,0:T(8,128)(2,1)S(1)}, bf16[2,1,128,4096]{3,2,1,0:T(8,128)(2,1)}, u32[]{:S(2)}) copy-start(bf16[2,1,128,4096]{3,2,1,0:T(8,128)(2,1)} %param.15) | copy-start | bytes 6291460
Sparse Core Ops, SparseCore 0:
  10.9 113.7 all-gather.2
  128.3 85.5 all-gather.4
where the time goes:
time: 637 us; the launch traced here: 636 us
  waiting for transfers between devices  216 us (34%)
  local copies, waits for them, and re-layouts  193 us (30%)
  blocking collectives  149 us (23%)
  matrix products  35.8 us (6%)
  other arithmetic  15.8 us (2%)
  between operations  13.5 us (2%)
  starting transfers between devices  11.7 us (2%)
    ppermute x9, waiting for transfers between devices, shifted(): lax.ppermute(value, axis, [(source, source + steps) for source in range(l...  214 us
    gather x4, local copies, waits for them, and re-layouts, band_pair(): kernel[:, jnp.clip(offset, 0, taps - 1)]  155 us
    all_gather x1, blocking collectives, shards(): lax.all_gather(filters, 'dp', axis=1, tiled=True)  121 us
    psum x1, blocking collectives, shards(): return lax.psum(feats_done, 'section')  28.1 us
    dot_general x4, matrix products, spread_back(): jnp.einsum('gtu,bugc->btgc', within, blocks, preferred_element_type=jnp.f...  22.4 us
    dynamic_slice x18, local copies, waits for them, and re-layouts, tick(): top_now = lax.dynamic_index_in_dim(top_cot, slot_clip, 0, keepdims=False)  17.8 us
  transfers between devices with their start and end apart: 11, of which 9 were waited for; matrix products, arithmetic and copies ran while one was open for 29% of the time, Pallas kernels for 0%

commit v1 on v0

v1 whole, which is shorter than its diff:
```python
import functools
import jax
import jax.numpy as jnp
from jax import lax
from jax.sharding import PartitionSpec as P
from jax.experimental import pallas as pl
from jax.experimental.pallas import tpu as pltpu

BF = jnp.bfloat16
F32 = jnp.float32
CHUNKS = 2
PIECES = ((0, 512), (512, 512))
VMEM = 16 * 1024 * 1024
PARAMS = dict(compiler_params=pltpu.CompilerParams(vmem_limit_bytes=VMEM))


def swap(value, axis, bit):
    count = lax.axis_size(axis)
    return lax.ppermute(value, axis, [(i, i ^ bit) for i in range(count)])


def after(value, *others):
    return lax.optimization_barrier((value, others))[0]


def whole(shape):
    return pl.BlockSpec(shape, lambda *ids: (0,) * len(shape))


def held(count):
    return [pl.BlockSpec(memory_space=pltpu.VMEM)] * count


def paired(ref, block):
    return jnp.concatenate(
        [ref[:, block * 256 : block * 256 + 256], ref[:, 2048 + block * 256 : 2304 + block * 256]], axis=1
    )


def sort_matrix(quarters):
    row = lax.broadcasted_iota(jnp.int32, (512, 128), 0)
    col = lax.broadcasted_iota(jnp.int32, (512, 128), 1)
    tile = (col // 32) % 2 * 2 + col // 64
    return jnp.concatenate([(row == tile * 128 + quarter * 32 + col % 32).astype(BF) for quarter in quarters], axis=1)


def gates_body(gate_ref, sort_ref, *outs):
    for block in range(8):
        picked = jnp.dot(paired(gate_ref, block), sort_ref[...], preferred_element_type=F32).astype(BF)
        for number in range(4):
            for piece, (start, size) in enumerate(PIECES):
                lane = block * 128 - start
                if 0 <= lane < size:
                    outs[number * 2 + piece][:, lane : lane + 128] = picked[:, number * 128 : number * 128 + 128]


def sort_gates(gates, matrix):
    sizes = [size for _ in range(4) for _, size in PIECES]
    return pl.pallas_call(
        gates_body,
        grid=(2,),
        in_specs=[pl.BlockSpec((256, 4096), lambda i: (i, 0)), whole((512, 512))],
        out_specs=[pl.BlockSpec((256, size), lambda i: (i, 0)) for size in sizes],
        out_shape=[jax.ShapeDtypeStruct((512, size), BF) for size in sizes],
        name="sort_gates",
        compiler_params=pltpu.CompilerParams(vmem_limit_bytes=56 * 1024 * 1024),
    )(gates, matrix)


def hidden_body(hidden_ref, sort_ref, out_ref):
    for block in range(8):
        out_ref[:, block * 128 : block * 128 + 128] = jnp.dot(
            paired(hidden_ref, block), sort_ref[...], preferred_element_type=F32
        ).astype(BF)


def pick_hidden(hidden, matrix):
    return pl.pallas_call(
        hidden_body,
        in_specs=held(2),
        out_specs=held(1)[0],
        out_shape=jax.ShapeDtypeStruct((256, 1024), BF),
        name="pick_hidden",
        **PARAMS,
    )(hidden, matrix)


def logits_body(place_ref, hidden_ref, vocab_ref, keep_ref, send_ref, total_ref):
    total = jnp.zeros((256, 512), F32)
    for block in range(4):
        weights = jnp.concatenate(
            [
                vocab_ref[block * 8 : block * 8 + 8, part * 32 : part * 32 + 32, :].reshape(256, 128)
                for part in range(4)
            ],
            axis=1,
        )
        total = total + jnp.dot(
            hidden_ref[:, block * 256 : block * 256 + 256], weights, preferred_element_type=F32
        )
    total_ref[...] = total
    core = place_ref[1]
    keep_ref[...] = total_ref[pl.ds(pl.multiple_of(core * 128, 128), 128), :]
    send_ref[...] = total_ref[pl.ds(pl.multiple_of((1 - core) * 128, 128), 128), :]


def partial_logits(place, hidden, gathered):
    return pl.pallas_call(
        logits_body,
        in_specs=[pl.BlockSpec(memory_space=pltpu.SMEM)] + held(2),
        out_specs=held(2),
        out_shape=[jax.ShapeDtypeStruct((128, 512), F32)] * 2,
        scratch_shapes=[pltpu.VMEM((256, 512), F32)],
        name="partial_logits",
        **PARAMS,
    )(place, hidden, gathered)


def top_body(dlogits_ref, vocab_ref, out_ref):
    total = jnp.zeros((256, 256), F32)
    for part in range(4):
        weights = vocab_ref[:, part * 32 : part * 32 + 32, :].reshape(256, 128)
        total = total + lax.dot_general(
            dlogits_ref[:, part * 128 : part * 128 + 128], weights, (((1,), (1,)), ((), ())), preferred_element_type=F32
        )
    out_ref[...] = total.astype(BF)


def top_cotangent(dlogits, gathered):
    return pl.pallas_call(
        top_body,
        grid=(4,),
        in_specs=[
            whole((256, 512)),
            pl.BlockSpec((8, 128, 128), lambda i: (i, 0, 0)),
        ],
        out_specs=pl.BlockSpec((256, 256), lambda i: (0, i)),
        out_shape=jax.ShapeDtypeStruct((256, 1024), BF),
        name="top_cotangent",
        **PARAMS,
    )(dlogits, gathered)


def toeplitz(row):
    spread = jnp.broadcast_to(row, (128, 128))
    turned = pltpu.roll(spread, 0, 1, stride=1, stride_axis=0)
    earlier = lax.broadcasted_iota(jnp.int32, (128, 128), 0)
    later = lax.broadcasted_iota(jnp.int32, (128, 128), 1)
    return jnp.where(later >= earlier, turned, 0.0).astype(BF)


def piece_of(chunk):
    return max(number for number, (start, _) in enumerate(PIECES) if start <= chunk * 1024 // CHUNKS)


def layer_step(layer, place, cot_ref, gate_refs, filt_ref, chunk, tiles):
    zx = (layer // 4) ^ place[0]
    cx = (layer // 2 % 2) ^ place[1]
    lane = lax.broadcasted_iota(jnp.int32, (128, 256), 1) % 128
    odd = lane // 16 % 2 == 1
    for tile in range(tiles):
        lanes = slice(tile * 128, tile * 128 + 128)
        inside = (chunk * tiles + tile) * 128 - PIECES[piece_of(chunk)][0]
        gate_lanes = slice(inside, inside + 128)
        scaled = []
        olds = []
        for micro in range(2):
            rows = pl.ds(pl.multiple_of(layer % 2 * 256 + micro * 128, 128), 128)
            near, side, over, cross = [ref[rows, gate_lanes] for ref in gate_refs]
            gate = jnp.where(zx == 0, jnp.where(cx == 0, near, side), jnp.where(cx == 0, over, cross))
            old = cot_ref[micro * 128 : micro * 128 + 128, lanes].astype(F32)
            olds.append(old)
            scaled.append((gate.astype(F32) * old).astype(BF))
        values = jnp.concatenate(scaled, axis=1)
        none = jnp.zeros_like(values)
        split = jnp.concatenate([jnp.where(odd, none, values), jnp.where(odd, values, none)], axis=0)
        kept = None
        for pair in range(4):
            first = (chunk * tiles + tile) * 8 + pair * 2
            band = jnp.concatenate(
                [toeplitz(filt_ref[layer, first : first + 1, :]), toeplitz(filt_ref[layer, first + 1 : first + 2, :])],
                axis=1,
            )
            back = jnp.dot(band, split, preferred_element_type=F32)
            kept = back if pair == 0 else jnp.where(lane // 32 == pair, back, kept)
        for micro in range(2):
            cot_ref[micro * 128 : micro * 128 + 128, lanes] = (
                olds[micro] + kept[:, micro * 128 : micro * 128 + 128]
            ).astype(BF)


def upper_body(chunk, width, place_ref, cot_ref, near, side, over, cross, filt_ref, out_ref):
    place = (place_ref[0], place_ref[1])
    out_ref[...] = cot_ref[:, chunk * width : chunk * width + width]

    def step(i, carry):
        layer_step(7 - i, place, out_ref, (near, side, over, cross), filt_ref, chunk, width // 128)
        return carry

    lax.fori_loop(0, 8, step, 0)


def lower_body(
    chunk, width, place_ref, top_ref, recv_ref, near, side, over, cross, filt_ref, basis_ref, out_ref, cot_ref
):
    place = (place_ref[0], place_ref[1])
    is_top = place_ref[2] == 1
    cot_ref[...] = jnp.where(is_top, top_ref[:, chunk * width : chunk * width + width], recv_ref[...])
    lane = lax.broadcasted_iota(jnp.int32, (256, 128), 1)

    def project(layer):
        slot = ((layer // 4) ^ place[0]) * 2 + ((layer // 2 % 2) ^ place[1])
        rows = pl.ds(pl.multiple_of(slot * 32, 32), 32)
        weights = basis_ref[chunk * (width // 32) : (chunk + 1) * (width // 32), rows, :].reshape(width, 128)
        made = jnp.dot(cot_ref[...], weights, preferred_element_type=F32)
        out_ref[slot] = jnp.where(lane // 64 == layer % 2, made, out_ref[slot])

    def step(i, carry):
        project(7 - i)
        layer_step(7 - i, place, cot_ref, (near, side, over, cross), filt_ref, chunk, width // 128)
        return carry

    out_ref[...] = jnp.zeros_like(out_ref)
    lax.fori_loop(0, 7, step, 0)
    project(0)


def upper(chunk, width, place, cot, gate_set, filt):
    return pl.pallas_call(
        functools.partial(upper_body, chunk, width),
        in_specs=[pl.BlockSpec(memory_space=pltpu.SMEM)] + held(6),
        out_specs=held(1)[0],
        out_shape=jax.ShapeDtypeStruct((256, width), BF),
        name="upper",
        **PARAMS,
    )(place, cot, *gate_set, filt)


def lower(chunk, width, place, cot, received, gate_set, filt, gathered):
    return pl.pallas_call(
        functools.partial(lower_body, chunk, width),
        in_specs=[pl.BlockSpec(memory_space=pltpu.SMEM)] + held(8),
        out_specs=held(1)[0],
        out_shape=jax.ShapeDtypeStruct((4, 256, 128), F32),
        scratch_shapes=[pltpu.VMEM((256, width), BF)],
        name="lower",
        **PARAMS,
    )(place, cot, received, *gate_set, filt, gathered)


def rows_in_body(acts_ref, basis_ref, out_ref):
    lane = lax.broadcasted_iota(jnp.int32, (256, 128), 1)
    made = []
    for layer in range(2):
        total = jnp.zeros((256, 128), F32)
        for block in range(16):
            left = acts_ref[layer, :, block * 128 : block * 128 + 128]
            right = acts_ref[layer, :, 2048 + block * 128 : 2176 + block * 128]
            weights = basis_ref[block * 2 : block * 2 + 2, 128:256, :].reshape(256, 128)
            total = total + jnp.dot(jnp.concatenate([left, right], axis=1), weights, preferred_element_type=F32)
        made.append(total)
    out_ref[...] = jnp.where(lane < 64, made[0], made[1])


def project_in(acts, gathered):
    return pl.pallas_call(
        rows_in_body,
        in_specs=held(2),
        out_specs=held(1)[0],
        out_shape=jax.ShapeDtypeStruct((256, 128), F32),
        name="rows_in",
        **PARAMS,
    )(acts, gathered)


def term_body(*refs):
    parts, rows_in_ref, out_ref = refs[:-2], refs[-2], refs[-1]
    for micro in range(2):
        rows = slice(micro * 128, micro * 128 + 128)
        total = jnp.zeros((128, 128), F32)
        for slot in range(4):
            rows_out = parts[0][slot, rows, :]
            for part in parts[1:]:
                rows_out = rows_out + part[slot, rows, :]
            total = total + lax.dot_general(
                rows_out,
                rows_in_ref[slot, rows, :],
                (((0,), (0,)), ((), ())),
                preferred_element_type=F32,
                precision=lax.Precision.HIGHEST,
            )
        out_ref[:, micro * 64 : micro * 64 + 64] = total[:64, :64] + total[64:, 64:]


def terms(parts, rows_in):
    return pl.pallas_call(
        term_body,
        in_specs=held(len(parts) + 1),
        out_specs=held(1)[0],
        out_shape=jax.ShapeDtypeStruct((64, 128), F32),
        name="terms",
        **PARAMS,
    )(*parts, rows_in)


def with_other(value):
    other = swap(value, "dp", 16)
    high = lax.axis_index("dp") // 16
    return jnp.where(high == 0, jnp.stack([value, other]), jnp.stack([other, value]))


def gather_xy(both):
    groups = [list(range(16)), list(range(16, 32))]
    spread = jnp.broadcast_to(both[None], (16,) + both.shape)
    out = lax.all_to_all(spread, "dp", 0, 0, axis_index_groups=groups)
    return out.reshape((32,) + both.shape[1:])


def shards(acts, gates, filters, bases, final_hidden, unembed, targets):
    section = lax.axis_index("section")
    core = section % 2
    zbit = section // 2 % 2
    place = jnp.stack([zbit, core, section // 4, section]).astype(jnp.int32)
    quarter = 2 * core + zbit

    def pick(value, index, count, axis=0):
        return lax.dynamic_slice_in_dim(value, index, count, axis)

    matrix = sort_matrix([quarter, 2 * core + 1 - zbit, 2 * (1 - core) + zbit, 2 * (1 - core) + 1 - zbit])
    gate_out = sort_gates(gates.reshape(512, 4096), matrix)
    near, far, side_send, cross_send = [gate_out[number * 2 : number * 2 + 2] for number in range(4)]
    unembed, bases, filters = after((unembed, bases, filters), gate_out)
    sides = [swap(value, "section", 1) for value in side_send]
    crosses = [swap(value, "section", 1) for value in cross_send]

    def vocab_rows(which):
        return pick(unembed, which * 32, 32).reshape(32, 4, 128).transpose(1, 0, 2).reshape(128, 128)

    high = lax.axis_index("dp") // 16
    mirror = [(s * 32 + d, (s ^ 6) * 32 + (d ^ 16)) for s in range(8) for d in range(32)]
    other = lax.ppermute(vocab_rows(2 * core + 1 - zbit), ("section", "dp"), mirror)
    mine = vocab_rows(quarter)
    vocab_both = jnp.where(high == 0, jnp.stack([mine, other]), jnp.stack([other, mine]))

    out_rows = jnp.concatenate([bases[0, :, 64:], bases[1, :, 64:]], axis=1).reshape(4, 32, 128)
    filt_rows = filters.reshape(2, 4, 2, 128).transpose(1, 0, 2, 3).reshape(4, 4, 128)
    small = jnp.concatenate([out_rows, filt_rows], axis=1)
    side = swap(pick(small, 2 * (1 - core), 2), "section", 1)
    chip = jnp.stack([pick(small, 2 * core, 2), side], axis=1)
    over = swap(pick(chip, 1 - zbit, 1)[0], "section", 2)
    slots = jnp.concatenate([pick(chip, zbit, 1)[0], over], axis=0)
    out_slots = slots[:, :32].reshape(128, 128)
    filt_slots = slots[:, 32:].reshape(16, 128)
    in_rows = jnp.concatenate([bases[0, :, :64], bases[1, :, :64]], axis=1)
    slots_both = with_other(jnp.concatenate([out_slots, in_rows, filt_slots], axis=0))

    hidden = pick_hidden(final_hidden.reshape(256, 4096), sort_matrix([quarter]))
    late = swap(far[1], "section", 2)
    vocab_both, slots_both, far, crosses, hidden, late = lax.optimization_barrier(
        (vocab_both, slots_both, far, crosses, hidden, late)
    )
    overs = [swap(far[0], "section", 2), late]
    crossed = [swap(crosses[0], "section", 2)]
    first = gather_xy(jnp.concatenate([vocab_both, slots_both[:, 256:]], axis=1))
    second = gather_xy(after(slots_both[:, :256], first))

    filt = first[:, 128:, :].astype(F32).reshape(32, 2, 2, 2, 2, 128)
    filt = jnp.where(zbit == 0, filt, filt[:, ::-1])
    filt = jnp.where(core == 0, filt, filt[:, :, ::-1])
    filt = filt.transpose(1, 2, 3, 0, 4, 5).reshape(8, 64, 128)

    keep, send = partial_logits(place, hidden, first)
    half = keep + swap(send, "section", 1)
    half = after(half, overs[0], crossed[0])
    rows = pick(half, zbit * 64, 64) + swap(pick(half, (1 - zbit) * 64, 64), "section", 2)
    ids = pick(targets.reshape(256), core * 128 + zbit * 64, 64)
    exps = jnp.exp(rows - jnp.max(rows, axis=1, keepdims=True))
    probs = exps / jnp.sum(exps, axis=1, keepdims=True)
    onehot = (ids[:, None] == jnp.arange(512)[None, :]).astype(F32)
    mine = (probs - onehot).astype(BF)
    other = swap(mine, "section", 2)
    crossed.append(swap(after(crosses[1], other), "section", 2))
    gate_sets = [(near[piece], sides[piece], overs[piece], crossed[piece]) for piece in range(2)]
    mine = jnp.where(zbit == 0, jnp.concatenate([mine, other]), jnp.concatenate([other, mine]))
    other = swap(mine, "section", 1)
    dlogits = jnp.where(core == 0, jnp.concatenate([mine, other]), jnp.concatenate([other, mine]))
    top = top_cotangent(dlogits, first)

    width = 1024 // CHUNKS
    received = []
    for chunk in range(CHUNKS):
        start = after(top, passed) if chunk else top
        passed = upper(chunk, width, place, start, gate_sets[piece_of(chunk)], filt)
        received.append(lax.ppermute(passed, "section", [(s, s - 4) for s in range(4, 8)]))

    start = after(received[0], passed)
    parts = [lower(0, width, place, top, start, gate_sets[0], filt, second)]
    rows_in = project_in(acts.reshape(2, 256, 4096), after(second, parts[0], received[1]))
    start = after(received[1], rows_in)
    parts.append(lower(1, width, place, top, start, gate_sets[1], filt, second))
    rows_in = jnp.stack([rows_in, swap(rows_in, "section", 1)])
    rows_in = jnp.concatenate([rows_in, swap(rows_in, "section", 2)], axis=0)
    feats = terms(parts, rows_in)
    feats = feats + swap(feats, "section", 1)
    feats = (feats + swap(feats, "section", 2)) + (swap(feats, "section", 4) + swap(feats, "section", 6))
    return feats.reshape(64, 2, 64).transpose(1, 0, 2).reshape(2, 1, 4096)


def solution(mesh):
    in_specs = (
        P("section", None, "dp", None, None),
        P("section", None, "dp", None, None),
        P("section", "dp", None),
        P("section", "dp", None),
        P(None, "dp", None, None),
        P("dp", None),
        P(None, "dp", None),
    )
    return jax.shard_map(shards, mesh=mesh, in_specs=in_specs, out_specs=P(None, "dp", None), check_vma=False)
```

time: 637 us -> 144 us (0.23)
  local copies, waits for them, and re-layouts: 193 us -> 7.75 us
  waiting for transfers between devices: 216 us -> 49.9 us
  blocking collectives: 149 us -> 0 us
  matrix products: 35.8 us -> 0 us
  Pallas kernels: 0 us -> 34.1 us
  starting transfers between devices: 11.7 us -> 45.1 us
  between operations: 13.5 us -> 0.63 us
  other arithmetic: 15.8 us -> 4.13 us
    ppermute x9 -> x24, waiting for transfers between devices: 214 us -> 38.4 us  [the longest x21 26.4 us: swap(): return lax.ppermute(value, axis, [(i, i ^ bit) for i in range(count)])]
    gather x4 -> x0, local copies, waits for them, and re-layouts: 155 us -> none  [band_pair(): kernel[:, jnp.clip(offset, 0, taps - 1)]]
    all_gather x1 -> x0, blocking collectives: 121 us -> none  [shards(): lax.all_gather(filters, 'dp', axis=1, tiled=True)]
    dot_general x18 -> x0, matrix products: 35.8 us -> none  [the longest x4 22.4 us: spread_back(): jnp.einsum('gtu,bugc->btgc', within, blocks, preferred_element_type=jnp.f...]
    pallas_call x0 -> x10, Pallas kernels: none -> 34.1 us  [the longest x2 11.7 us: upper(): pl.pallas_call(functools.partial(upper_body, chunk, width), in_specs=[pl....]
    psum x1 -> x0, blocking collectives: 28.1 us -> none  [shards(): return lax.psum(feats_done, 'section')]
    ppermute x9 -> x24, starting transfers between devices: 11.6 us -> 34.7 us  [the longest x21 27.1 us: swap(): return lax.ppermute(value, axis, [(i, i ^ bit) for i in range(count)])]
    dynamic_slice x18 -> x4, local copies, waits for them, and re-layouts: 17.8 us -> 0.11 us  [pick(): return lax.dynamic_slice_in_dim(value, index, count, axis)]
  transfers between devices with their start and end apart: 11 -> 26, of which waited for: 9 -> 14; matrix products, arithmetic and copies ran while one was open for 29% -> 4% of each run, Pallas kernels for 0% -> 19%
where the time goes in v1:
time: 144 us; the launch traced here: 142 us
  waiting for transfers between devices  49.9 us (35%)
  starting transfers between devices  45.1 us (31%)
  Pallas kernels  34.1 us (24%)
  local copies, waits for them, and re-layouts  7.75 us (5%)
  other arithmetic  4.13 us (3%)
    ppermute x21, starting transfers between devices, swap(): return lax.ppermute(value, axis, [(i, i ^ bit) for i in range(count)])  27.1 us
    ppermute x21, waiting for transfers between devices, swap(): return lax.ppermute(value, axis, [(i, i ^ bit) for i in range(count)])  26.4 us
    ppermute x2, waiting for transfers between devices, shards(): lax.ppermute(passed, 'section', [(s, s - 4) for s in range(4, 8)])  12 us
    pallas_call x2, Pallas kernels, upper(): pl.pallas_call(functools.partial(upper_body, chunk, width), in_specs=[pl....  11.7 us
    all_to_all x2, waiting for transfers between devices, gather_xy(): out = lax.all_to_all(spread, 'dp', 0, 0, axis_index_groups=groups)  11.5 us
    pallas_call x2, Pallas kernels, lower(): pl.pallas_call(functools.partial(lower_body, chunk, width), in_specs=[pl....  10.9 us
    all_to_all x2, starting transfers between devices, gather_xy(): out = lax.all_to_all(spread, 'dp', 0, 0, axis_index_groups=groups)  10.4 us
    pallas_call x1, Pallas kernels, sort_gates(): pl.pallas_call(gates_body, grid=(2,), in_specs=[pl.BlockSpec((256, 4096),...  5.64 us
  transfers between devices with their start and end apart: 26, of which 14 were waited for; matrix products, arithmetic and copies ran while one was open for 4% of the time, Pallas kernels for 19%

profile of v1, /device:TPU:0, one launch (start us, length us, event | category | flops | bytes accessed | tf_op | source)
XLA Modules:
  0.0 141.7 jit_solution(8638554102649836941)
XLA Ops:
  0.2 0.9 pad_maximum_fusion.sort_ref
  1.1 5.6 %sort_gates.1 = (bf16[512,512]{1,0:T(8,128)(2,1)}, bf16[512,512]{1,0:T(8,128)(2,1)}, bf16[512,512]{1,0:T(8,128)(2,1)}, bf16[512,512]{1,0:T(8,128)(2,1)}, bf16[51...) custom-call(bf16[512,4096]{1,0:T(8,128)(2,1)} %bitcast.60, ...), custom_call_target="tpu_custom_call" | custom-call | tf_op jit(solution)/shard_map/sort_gates/pallas_call | solution.py:59
  6.8 0.5 collective-permute-start.5
  7.9 5.0 %collective-permute-start = (bf16[128,128]{1,0:T(8,128)(2,1)S(1)}, bf16[128,128]{1,0:T(8,128)(2,1)S(1)}, u32[]{:S(2)}, u32[]{:S(2)}) collective-permute-start(bf16[128,128]{1,0:T(8,128)(2,1)S(1)} %bitcast.75), channel_id=1, source_target_pairs={{0,208},{1,209},{2,210},{3,211},{4,212},{5,213},{6,214},{7,215},{8... | collective-permute-start | bytes 98312 | tf_op jit(solution)/shard_map/ppermute | solution.py:341
  12.9 0.7 pick_hidden.1.hidden_ref
  13.6 0.8 copy-done.12
  14.5 2.0 %collective-permute-start.2 = (bf16[2,36,128]{2,1,0:T(8,128)(2,1)S(1)}, bf16[2,36,128]{2,1,0:T(8,128)(2,1)S(1)}, u32[]{:S(2)}, u32[]{:S(2)}) collective-permute-start(bf16[2,36,128]{2,1,0:T(8,128)(2,1)S(1)} %get-tuple-element.68), channel_id=1, source_target_pairs={{0,64},{32,96},{64,0},{96,32},{128,192},{160,224},{192,128},{224,1... | collective-permute-start | bytes 55304 | tf_op jit(solution)/shard_map/ppermute | solution.py:19
  16.5 6.0 %collective-permute-done.2 = bf16[2,36,128]{2,1,0:T(8,128)(2,1)S(1)} collective-permute-done((bf16[2,36,128]{2,1,0:T(8,128)(2,1)S(1)}, bf16[2,36,128]{2,1,0:T(8,128)(2,1)S(1)}, u32[]{:S(2)}, u32[]{:S(2)}) %collective-permute-start.2) | collective-permute-done | bytes 18464 | tf_op jit(solution)/shard_map/ppermute | solution.py:19
  22.7 5.5 %collective-permute-start.3 = (bf16[272,128]{1,0:T(8,128)(2,1)S(1)}, bf16[272,128]{1,0:T(8,128)(2,1)S(1)}, u32[]{:S(2)}, u32[]{:S(2)}) collective-permute-start(bf16[272,128]{1,0:T(8,128)(2,1)S(1)} %pad_maximum_fusion.4), channel_id=1, source_target_pairs={{0,16},{1,17},{2,18},{3,19},{4,20},{5,21},{6,22},{7,23},{8,24},{9,... | collective-permute-start | bytes 208904 | tf_op jit(solution)/shard_map/ppermute | solution.py:19
  28.3 2.7 %collective-permute-done.3 = bf16[272,128]{1,0:T(8,128)(2,1)S(1)} collective-permute-done((bf16[272,128]{1,0:T(8,128)(2,1)S(1)}, bf16[272,128]{1,0:T(8,128)(2,1)S(1)}, u32[]{:S(2)}, u32[]{:S(2)}) %collective-permute-start.3) | collective-permute-done | bytes 69664 | tf_op jit(solution)/shard_map/ppermute | solution.py:19
  31.0 1.2 broadcast_in_dim.4
  32.3 6.6 %all-to-all-start = ((bf16[16,2,144,128]{3,2,1,0:T(8,128)(2,1)}), bf16[16,2,144,128]{3,2,1,0:T(8,128)(2,1)S(1)}, u32[]{:S(2)}, u32[]{:S(2)}) async-start(bf16[16,2,144,128]{3,2,1,0:T(8,128)(2,1)} %broadcast_in_dim.4), calls=%async_computation | async-start | bytes 2359296 | tf_op jit(solution)/shard_map/all_to_all | solution.py:315
  38.9 5.4 %collective-permute-start.8 = (bf16[512,512]{1,0:T(8,128)(2,1)}, bf16[512,512]{1,0:T(8,128)(2,1)}, u32[]{:S(2)}, u32[]{:S(2)}) collective-permute-start(bf16[512,512]{1,0:T(8,128)(2,1)} %get-tuple-element.48), channel_id=1, source_target_pairs={{0,64},{32,96},{64,0},{96,32},{128,192},{160,224},{192,128},{224,1... | collective-permute-start | bytes 1572872 | tf_op jit(solution)/shard_map/ppermute | solution.py:19
  44.4 11.5 %all-to-all-done = bf16[16,2,144,128]{3,2,1,0:T(8,128)(2,1)S(1)} async-done(((bf16[16,2,144,128]{3,2,1,0:T(8,128)(2,1)}), bf16[16,2,144,128]{3,2,1,0:T(8,128)(2,1)S(1)}, u32[]{:S(2)}, u32[]{:S(2)}) %all-to-all-start) | async-done | bytes 1179680 | tf_op jit(solution)/shard_map/all_to_all | solution.py:315
  55.9 1.7 %partial_logits.1 = (f32[128,512]{1,0:T(8,128)S(1)}, f32[128,512]{1,0:T(8,128)}) custom-call(s32[4]{0:T(128)S(1)} %pad_add_fusion.place_ref, bf16[256,1024]{1,0:T(8,128)(2,1)S(1)} %copy-done.13, bf16[32,144,128]{2,1,0:T(8,128)(2,1)S(1)} %bitcast.49), custom_call_target="tpu_custom_call" | custom-call | tf_op jit(solution)/shard_map/partial_logits/pallas_call | solution.py:108
  57.7 1.8 %broadcast_in_dim.5 = bf16[16,2,256,128]{3,2,1,0:T(8,128)(2,1)} broadcast(bf16[2,256,128]{2,1,0:T(8,128)(2,1)S(1)} %slice.35), dimensions={1,2,3} | broadcast | bytes 2228224 | tf_op jit(solution)/shard_map/broadcast_in_dim | solution.py:314
  59.5 3.8 %all-to-all-start.1 = ((bf16[16,2,256,128]{3,2,1,0:T(8,128)(2,1)}), bf16[16,2,256,128]{3,2,1,0:T(8,128)(2,1)S(1)}, u32[]{:S(2)}, u32[]{:S(2)}) async-start(bf16[16,2,256,128]{3,2,1,0:T(8,128)(2,1)} %broadcast_in_dim.5), calls=%async_computation.1 | async-start | bytes 4194304 | tf_op jit(solution)/shard_map/all_to_all | solution.py:315
  63.4 1.0 add.185
  64.4 1.6 %collective-permute-done.9.cross = bf16[512,512]{1,0:T(8,128)(2,1)} collective-permute-done((bf16[512,512]{1,0:T(8,128)(2,1)}, bf16[512,512]{1,0:T(8,128)(2,1)}, u32[]{:S(2)}, u32[]{:S(2)}) %collective-permute-start.9) | collective-permute-done | bytes 524320 | tf_op jit(solution)/shard_map/ppermute | solution.py:19
  66.0 4.5 %collective-permute-start.10 = (f32[64,512]{1,0:T(8,128)S(1)}, f32[64,512]{1,0:T(8,128)S(1)}, u32[]{:S(2)}, u32[]{:S(2)}) collective-permute-start(f32[64,512]{1,0:T(8,128)S(1)} %constant_dynamic-slice_fusion), channel_id=1, source_target_pairs={{0,64},{32,96},{64,0},{96,32},{128,192},{160,224},{192,128},{224,1... | collective-permute-start | bytes 393224 | tf_op jit(solution)/shard_map/ppermute | solution.py:19
  71.0 3.6 %collective-permute-done.10 = f32[64,512]{1,0:T(8,128)S(1)} collective-permute-done((f32[64,512]{1,0:T(8,128)S(1)}, f32[64,512]{1,0:T(8,128)S(1)}, u32[]{:S(2)}, u32[]{:S(2)}) %collective-permute-start.10) | collective-permute-done | bytes 131104 | tf_op jit(solution)/shard_map/ppermute | solution.py:19
  74.6 1.0 fusion.18
  76.0 1.8 %collective-permute-start.11 = (bf16[64,512]{1,0:T(8,128)(2,1)S(1)}, bf16[64,512]{1,0:T(8,128)(2,1)S(1)}, u32[]{:S(2)}, u32[]{:S(2)}) collective-permute-start(bf16[64,512]{1,0:T(8,128)(2,1)S(1)} %subtract_convert_fusion), channel_id=1, source_target_pairs={{0,64},{32,96},{64,0},{96,32},{128,192},{160,224},{192,128},{224,1... | collective-permute-start | bytes 196616 | tf_op jit(solution)/shard_map/ppermute | solution.py:19
  77.9 2.4 %collective-permute-done.11 = bf16[64,512]{1,0:T(8,128)(2,1)S(1)} collective-permute-done((bf16[64,512]{1,0:T(8,128)(2,1)S(1)}, bf16[64,512]{1,0:T(8,128)(2,1)S(1)}, u32[]{:S(2)}, u32[]{:S(2)}) %collective-permute-start.11) | collective-permute-done | bytes 65568 | tf_op jit(solution)/shard_map/ppermute | solution.py:19
  80.3 1.7 %collective-permute-start.16 = (bf16[512,512]{1,0:T(8,128)(2,1)}, bf16[512,512]{1,0:T(8,128)(2,1)S(1)}, u32[]{:S(2)}, u32[]{:S(2)}) collective-permute-start(bf16[512,512]{1,0:T(8,128)(2,1)} %collective-permute-done.5), channel_id=1, source_target_pairs={{0,64},{32,96},{64,0},{96,32},{128,192},{160,224},{192,128},{224,1... | collective-permute-start | bytes 1572872 | tf_op jit(solution)/shard_map/ppermute | solution.py:19
  82.4 1.2 collective-permute-done.12
  83.7 1.4 top_cotangent.1.cot_ref.top_ref
  85.1 5.6 %upper.2 = bf16[256,512]{1,0:T(8,128)(2,1)S(1)} custom-call(s32[4]{0:T(128)S(1)} %pad_add_fusion.place_ref, bf16[256,1024]{1,0:T(8,128)(2,1)S(1)} %top_cotangent.1.cot_ref.top_ref, bf16[512,512]{1,0:T(8,128)(2,1)S(1)} %copy-done.8, bf16[512,512]{1,0:T(8,128)(2,1)} %collective-permute-done.13.side, bf16[512,512]{1,0:T(8,128)(2,1)} %collective-permute-done.8.over, ...), custom_call_target="tpu_custom_call" | custom-call | tf_op jit(solution)/shard_map/upper/pallas_call | solution.py:229
  90.7 1.3 collective-permute-start.14
  92.0 1.4 %collective-permute-done.16.cross = bf16[512,512]{1,0:T(8,128)(2,1)S(1)} collective-permute-done((bf16[512,512]{1,0:T(8,128)(2,1)}, bf16[512,512]{1,0:T(8,128)(2,1)S(1)}, u32[]{:S(2)}, u32[]{:S(2)}) %collective-permute-start.16) | collective-permute-done | bytes 524320 | tf_op jit(solution)/shard_map/ppermute | solution.py:19
  93.4 6.1 %upper.3 = bf16[256,512]{1,0:T(8,128)(2,1)} custom-call(s32[4]{0:T(128)S(1)} %pad_add_fusion.place_ref, bf16[256,1024]{1,0:T(8,128)(2,1)S(1)} %top_cotangent.1.cot_ref.top_ref, bf16[512,512]{1,0:T(8,128)(2,1)S(1)} %copy-done.4, bf16[512,512]{1,0:T(8,128)(2,1)} %collective-permute-done.15.side, bf16[512,512]{1,0:T(8,128)(2,1)S(1)} %copy-done.6, ...), custom_call_target="tpu_custom_call" | custom-call | tf_op jit(solution)/shard_map/upper/pallas_call | solution.py:229
  99.6 1.3 collective-permute-start.17
  100.9 12.0 %collective-permute-done.14.recv_ref = bf16[256,512]{1,0:T(8,128)(2,1)S(1)} collective-permute-done((bf16[256,512]{1,0:T(8,128)(2,1)S(1)}, bf16[256,512]{1,0:T(8,128)(2,1)S(1)}, u32[]{:S(2)}, u32[]{:S(2)}) %collective-permute-start.14) | collective-permute-done | bytes 262176 | tf_op jit(solution)/shard_map/ppermute | solution.py:394
  112.9 0.7 copy-done.14
  113.5 1.0 copy-done.9
  114.6 0.9 copy-done.15
  115.5 5.7 %lower.2.refs_0_ = f32[4,256,128]{2,1,0:T(8,128)S(1)} custom-call(s32[4]{0:T(128)S(1)} %pad_add_fusion.place_ref, bf16[256,1024]{1,0:T(8,128)(2,1)S(1)} %top_cotangent.1.cot_ref.top_ref, bf16[256,512]{1,0:T(8,128)(2,1)S(1)} %copy-done.15, bf16[512,512]{1,0:T(8,128)(2,1)S(1)} %copy-done.9, bf16[512,512]{1,0:T(8,128)(2,1)} %collective-permute-done.13.side, ...), custom_call_target="tpu_custom_call" | custom-call | tf_op jit(solution)/shard_map/lower/pallas_call | solution.py:240
  121.2 1.3 rows_in.1
  122.6 1.3 collective-permute-done.18
  124.1 5.3 %lower.3.refs_1_ = f32[4,256,128]{2,1,0:T(8,128)S(1)} custom-call(s32[4]{0:T(128)S(1)} %pad_add_fusion.place_ref, bf16[256,1024]{1,0:T(8,128)(2,1)S(1)} %top_cotangent.1.cot_ref.top_ref, bf16[256,512]{1,0:T(8,128)(2,1)} %collective-permute-done.17.recv_ref, bf16[512,512]{1,0:T(8,128)(2,1)S(1)} %copy-done.4, bf16[512,512]{1,0:T(8,128)(2,1)} %collective-permute-done.15.side, ...), custom_call_target="tpu_custom_call" | custom-call | tf_op jit(solution)/shard_map/lower/pallas_call | solution.py:240
  129.4 3.0 %collective-permute-done.19 = f32[2,256,128]{2,1,0:T(8,128)S(1)} collective-permute-done((f32[2,256,128]{2,1,0:T(8,128)S(1)}, f32[2,256,128]{2,1,0:T(8,128)S(1)}, u32[]{:S(2)}, u32[]{:S(2)}) %collective-permute-start.19) | collective-permute-done | bytes 262176 | tf_op jit(solution)/shard_map/ppermute | solution.py:19
  132.5 0.8 terms.1
  133.3 1.2 collective-permute-done.20
  134.5 1.7 %collective-permute-start.22 = (f32[64,128]{1,0:T(8,128)S(1)}, f32[64,128]{1,0:T(8,128)S(1)}, u32[]{:S(2)}, u32[]{:S(2)}) collective-permute-start(f32[64,128]{1,0:T(8,128)S(1)} %add.191), channel_id=1, source_target_pairs={{0,128},{32,160},{64,192},{96,224},{128,0},{160,32},{192,64},{224,... | collective-permute-start | bytes 98312 | tf_op jit(solution)/shard_map/ppermute | solution.py:19
  136.3 2.6 %collective-permute-start.21 = (f32[64,128]{1,0:T(8,128)S(1)}, f32[64,128]{1,0:T(8,128)S(1)}, u32[]{:S(2)}, u32[]{:S(2)}) collective-permute-start(f32[64,128]{1,0:T(8,128)S(1)} %add.191), channel_id=1, source_target_pairs={{0,64},{32,96},{64,0},{96,32},{128,192},{160,224},{192,128},{224,1... | collective-permute-start | bytes 98312 | tf_op jit(solution)/shard_map/ppermute | solution.py:19
  138.9 1.6 %collective-permute-done.23 = f32[64,128]{1,0:T(8,128)S(1)} collective-permute-done((f32[64,128]{1,0:T(8,128)S(1)}, f32[64,128]{1,0:T(8,128)S(1)}, u32[]{:S(2)}, u32[]{:S(2)}) %collective-permute-start.23) | collective-permute-done | bytes 32800 | tf_op jit(solution)/shard_map/ppermute | solution.py:19
  140.5 0.3 collective-permute-done.21
  140.9 0.7 reshape.81
  (104 shorter events, 3.0 us)
Async XLA Ops:
  1.1 6.4 %copy-start.19 = (bf16[2,8,128]{2,1,0:T(8,128)(2,1)S(1)}, bf16[2,8,128]{2,1,0:T(8,128)(2,1)}, u32[]{:S(2)}) copy-start(bf16[2,8,128]{2,1,0:T(8,128)(2,1)} %param.9) | copy-start | bytes 12292
  1.1 6.4 %copy-start.17 = (bf16[2,128,128]{2,1,0:T(8,128)(2,1)S(1)}, bf16[2,128,128]{2,1,0:T(8,128)(2,1)}, u32[]{:S(2)}) copy-start(bf16[2,128,128]{2,1,0:T(8,128)(2,1)} %param.10) | copy-start | bytes 196612
  1.1 6.7 %copy-start.18 = (bf16[128,512]{1,0:T(8,128)(2,1)S(1)}, bf16[128,512]{1,0:T(8,128)(2,1)}, u32[]{:S(2)}) copy-start(bf16[128,512]{1,0:T(8,128)(2,1)} %param.12) | copy-start | bytes 393220
  1.1 11.8 %copy-start.3 = (bf16[2,1,128,4096]{3,2,1,0:T(8,128)(2,1)S(1)}, bf16[2,1,128,4096]{3,2,1,0:T(8,128)(2,1)}, u32[]{:S(2)}) copy-start(bf16[2,1,128,4096]{3,2,1,0:T(8,128)(2,1)} %param.11) | copy-start | bytes 6291460
  6.7 24.2 %collective-permute-start.4 = (bf16[512,512]{1,0:T(8,128)(2,1)}, bf16[512,512]{1,0:T(8,128)(2,1)}, u32[]{:S(2)}, u32[]{:S(2)}) collective-permute-start(bf16[512,512]{1,0:T(8,128)(2,1)} %get-tuple-element.38), channel_id=1, source_target_pairs={{0,32},{32,0},{64,96},{96,64},{128,160},{160,128},{192,224},{224,1... | collective-permute-start | bytes 1572872 | tf_op jit(solution)/shard_map/ppermute | solution.py:19
  6.8 24.2 %collective-permute-start.5 = (bf16[512,512]{1,0:T(8,128)(2,1)}, bf16[512,512]{1,0:T(8,128)(2,1)}, u32[]{:S(2)}, u32[]{:S(2)}) collective-permute-start(bf16[512,512]{1,0:T(8,128)(2,1)} %get-tuple-element.39), channel_id=1, source_target_pairs={{0,32},{32,0},{64,96},{96,64},{128,160},{160,128},{192,224},{224,1... | collective-permute-start | bytes 1572872 | tf_op jit(solution)/shard_map/ppermute | solution.py:19
  7.3 23.7 %collective-permute-start.6 = (bf16[512,512]{1,0:T(8,128)(2,1)}, bf16[512,512]{1,0:T(8,128)(2,1)S(1)}, u32[]{:S(2)}, u32[]{:S(2)}) collective-permute-start(bf16[512,512]{1,0:T(8,128)(2,1)} %get-tuple-element.35), channel_id=1, source_target_pairs={{0,64},{32,96},{64,0},{96,32},{128,192},{160,224},{192,128},{224,1... | collective-permute-start | bytes 1572872 | tf_op jit(solution)/shard_map/ppermute | solution.py:19
  7.7 6.8 %collective-permute-start.1 = (bf16[2,36,128]{2,1,0:T(8,128)(2,1)S(1)}, bf16[2,36,128]{2,1,0:T(8,128)(2,1)S(1)}, u32[]{:S(2)}, u32[]{:S(2)}) collective-permute-start(bf16[2,36,128]{2,1,0:T(8,128)(2,1)S(1)} %get-tuple-element.69), channel_id=1, source_target_pairs={{0,32},{32,0},{64,96},{96,64},{128,160},{160,128},{192,224},{224,1... | collective-permute-start | bytes 55304 | tf_op jit(solution)/shard_map/ppermute | solution.py:19
  7.9 8.6 %collective-permute-start = (bf16[128,128]{1,0:T(8,128)(2,1)S(1)}, bf16[128,128]{1,0:T(8,128)(2,1)S(1)}, u32[]{:S(2)}, u32[]{:S(2)}) collective-permute-start(bf16[128,128]{1,0:T(8,128)(2,1)S(1)} %bitcast.75), channel_id=1, source_target_pairs={{0,208},{1,209},{2,210},{3,211},{4,212},{5,213},{6,214},{7,215},{8... | collective-permute-start | bytes 98312 | tf_op jit(solution)/shard_map/ppermute | solution.py:341
  13.6 0.8 copy-start.12
  14.5 8.1 %collective-permute-start.2 = (bf16[2,36,128]{2,1,0:T(8,128)(2,1)S(1)}, bf16[2,36,128]{2,1,0:T(8,128)(2,1)S(1)}, u32[]{:S(2)}, u32[]{:S(2)}) collective-permute-start(bf16[2,36,128]{2,1,0:T(8,128)(2,1)S(1)} %get-tuple-element.68), channel_id=1, source_target_pairs={{0,64},{32,96},{64,0},{96,32},{128,192},{160,224},{192,128},{224,1... | collective-permute-start | bytes 55304 | tf_op jit(solution)/shard_map/ppermute | solution.py:19
  22.6 33.3 %copy-start.13 = (bf16[256,1024]{1,0:T(8,128)(2,1)S(1)}, bf16[256,1024]{1,0:T(8,128)(2,1)}, u32[]{:S(2)}) copy-start(bf16[256,1024]{1,0:T(8,128)(2,1)} %copy-done.12) | copy-start | bytes 1572868
  22.7 8.3 %collective-permute-start.3 = (bf16[272,128]{1,0:T(8,128)(2,1)S(1)}, bf16[272,128]{1,0:T(8,128)(2,1)S(1)}, u32[]{:S(2)}, u32[]{:S(2)}) collective-permute-start(bf16[272,128]{1,0:T(8,128)(2,1)S(1)} %pad_maximum_fusion.4), channel_id=1, source_target_pairs={{0,16},{1,17},{2,18},{3,19},{4,20},{5,21},{6,22},{7,23},{8,24},{9,... | collective-permute-start | bytes 208904 | tf_op jit(solution)/shard_map/ppermute | solution.py:19
  31.0 1.3 copy-start.5
  32.3 23.7 %all-to-all-start = ((bf16[16,2,144,128]{3,2,1,0:T(8,128)(2,1)}), bf16[16,2,144,128]{3,2,1,0:T(8,128)(2,1)S(1)}, u32[]{:S(2)}, u32[]{:S(2)}) async-start(bf16[16,2,144,128]{3,2,1,0:T(8,128)(2,1)} %broadcast_in_dim.4), calls=%async_computation | async-start | bytes 2359296 | tf_op jit(solution)/shard_map/all_to_all | solution.py:315
  38.9 25.5 %collective-permute-start.8 = (bf16[512,512]{1,0:T(8,128)(2,1)}, bf16[512,512]{1,0:T(8,128)(2,1)}, u32[]{:S(2)}, u32[]{:S(2)}) collective-permute-start(bf16[512,512]{1,0:T(8,128)(2,1)} %get-tuple-element.48), channel_id=1, source_target_pairs={{0,64},{32,96},{64,0},{96,32},{128,192},{160,224},{192,128},{224,1... | collective-permute-start | bytes 1572872 | tf_op jit(solution)/shard_map/ppermute | solution.py:19
  44.3 21.7 %collective-permute-start.9 = (bf16[512,512]{1,0:T(8,128)(2,1)}, bf16[512,512]{1,0:T(8,128)(2,1)}, u32[]{:S(2)}, u32[]{:S(2)}) collective-permute-start(bf16[512,512]{1,0:T(8,128)(2,1)} %collective-permute-done.4), channel_id=1, source_target_pairs={{0,64},{32,96},{64,0},{96,32},{128,192},{160,224},{192,128},{224,1... | collective-permute-start | bytes 1572872 | tf_op jit(solution)/shard_map/ppermute | solution.py:19
  55.9 21.9 %copy-start = (bf16[16,2,144,128]{3,2,1,0:T(8,128)(2,1)}, bf16[16,2,144,128]{3,2,1,0:T(8,128)(2,1)S(1)}, u32[]{:S(2)}) copy-start(bf16[16,2,144,128]{3,2,1,0:T(8,128)(2,1)S(1)} %all-to-all-done) | copy-start | bytes 3538948
  57.7 5.7 %collective-permute-start.7 = (f32[128,512]{1,0:T(8,128)}, f32[128,512]{1,0:T(8,128)}, u32[]{:S(2)}, u32[]{:S(2)}) collective-permute-start(f32[128,512]{1,0:T(8,128)} %get-tuple-element.47), channel_id=1, source_target_pairs={{0,32},{32,0},{64,96},{96,64},{128,160},{160,128},{192,224},{224,1... | collective-permute-start | bytes 786440 | tf_op jit(solution)/shard_map/ppermute | solution.py:19
  59.5 11.5 %copy-start.20 = (s32[2,1,128]{2,1,0:T(1,128)S(1)}, s32[2,1,128]{2,1,0:T(1,128)}, u32[]{:S(2)}) copy-start(s32[2,1,128]{2,1,0:T(1,128)} %param.13) | copy-start | bytes 3076
  59.5 54.0 %all-to-all-start.1 = ((bf16[16,2,256,128]{3,2,1,0:T(8,128)(2,1)}), bf16[16,2,256,128]{3,2,1,0:T(8,128)(2,1)S(1)}, u32[]{:S(2)}, u32[]{:S(2)}) async-start(bf16[16,2,256,128]{3,2,1,0:T(8,128)(2,1)} %broadcast_in_dim.5), calls=%async_computation.1 | async-start | bytes 4194304 | tf_op jit(solution)/shard_map/all_to_all | solution.py:315
  64.4 1.6 %copy-start.16 = (f32[128,512]{1,0:T(8,128)}, f32[128,512]{1,0:T(8,128)S(1)}, u32[]{:S(2)}) copy-start(f32[128,512]{1,0:T(8,128)S(1)} %add.185) | copy-start | bytes 786436
  66.0 8.6 %collective-permute-start.10 = (f32[64,512]{1,0:T(8,128)S(1)}, f32[64,512]{1,0:T(8,128)S(1)}, u32[]{:S(2)}, u32[]{:S(2)}) collective-permute-start(f32[64,512]{1,0:T(8,128)S(1)} %constant_dynamic-slice_fusion), channel_id=1, source_target_pairs={{0,64},{32,96},{64,0},{96,32},{128,192},{160,224},{192,128},{224,1... | collective-permute-start | bytes 393224 | tf_op jit(solution)/shard_map/ppermute | solution.py:19
  70.4 14.7 %collective-permute-start.13 = (bf16[512,512]{1,0:T(8,128)(2,1)}, bf16[512,512]{1,0:T(8,128)(2,1)}, u32[]{:S(2)}, u32[]{:S(2)}) collective-permute-start(bf16[512,512]{1,0:T(8,128)(2,1)} %get-tuple-element.36), channel_id=1, source_target_pairs={{0,32},{32,0},{64,96},{96,64},{128,160},{160,128},{192,224},{224,1... | collective-permute-start | bytes 1572872 | tf_op jit(solution)/shard_map/ppermute | solution.py:19
  70.7 21.3 %collective-permute-start.15 = (bf16[512,512]{1,0:T(8,128)(2,1)}, bf16[512,512]{1,0:T(8,128)(2,1)}, u32[]{:S(2)}, u32[]{:S(2)}) collective-permute-start(bf16[512,512]{1,0:T(8,128)(2,1)} %get-tuple-element.37), channel_id=1, source_target_pairs={{0,32},{32,0},{64,96},{96,64},{128,160},{160,128},{192,224},{224,1... | collective-permute-start | bytes 1572872 | tf_op jit(solution)/shard_map/ppermute | solution.py:19
  76.0 4.4 %collective-permute-start.11 = (bf16[64,512]{1,0:T(8,128)(2,1)S(1)}, bf16[64,512]{1,0:T(8,128)(2,1)S(1)}, u32[]{:S(2)}, u32[]{:S(2)}) collective-permute-start(bf16[64,512]{1,0:T(8,128)(2,1)S(1)} %subtract_convert_fusion), channel_id=1, source_target_pairs={{0,64},{32,96},{64,0},{96,32},{128,192},{160,224},{192,128},{224,1... | collective-permute-start | bytes 196616 | tf_op jit(solution)/shard_map/ppermute | solution.py:19
  77.8 5.9 %copy-start.1 = (bf16[16,2,144,128]{3,2,1,0:T(8,128)(2,1)S(1)}, bf16[16,2,144,128]{3,2,1,0:T(8,128)(2,1)}, u32[]{:S(2)}) copy-start(bf16[16,2,144,128]{3,2,1,0:T(8,128)(2,1)} %copy-done) | copy-start | bytes 3538948
  77.8 7.3 %copy-start.8 = (bf16[512,512]{1,0:T(8,128)(2,1)S(1)}, bf16[512,512]{1,0:T(8,128)(2,1)}, u32[]{:S(2)}) copy-start(bf16[512,512]{1,0:T(8,128)(2,1)} %get-tuple-element.32.near) | copy-start | bytes 1572868
  80.3 13.1 %collective-permute-start.16 = (bf16[512,512]{1,0:T(8,128)(2,1)}, bf16[512,512]{1,0:T(8,128)(2,1)S(1)}, u32[]{:S(2)}, u32[]{:S(2)}) collective-permute-start(bf16[512,512]{1,0:T(8,128)(2,1)} %collective-permute-done.5), channel_id=1, source_target_pairs={{0,64},{32,96},{64,0},{96,32},{128,192},{160,224},{192,128},{224,1... | collective-permute-start | bytes 1572872 | tf_op jit(solution)/shard_map/ppermute | solution.py:19
  82.2 1.4 %collective-permute-start.12 = (bf16[128,512]{1,0:T(8,128)(2,1)S(1)}, bf16[128,512]{1,0:T(8,128)(2,1)S(1)}, u32[]{:S(2)}, u32[]{:S(2)}) collective-permute-start(bf16[128,512]{1,0:T(8,128)(2,1)S(1)} %maximum_select_fusion.2), channel_id=1, source_target_pairs={{0,32},{32,0},{64,96},{96,64},{128,160},{160,128},{192,224},{224,1... | collective-permute-start | bytes 393224 | tf_op jit(solution)/shard_map/ppermute | solution.py:19
  83.7 9.7 %copy-start.4 = (bf16[512,512]{1,0:T(8,128)(2,1)S(1)}, bf16[512,512]{1,0:T(8,128)(2,1)}, u32[]{:S(2)}) copy-start(bf16[512,512]{1,0:T(8,128)(2,1)} %get-tuple-element.33.near) | copy-start | bytes 1572868
  83.7 9.7 %copy-start.6 = (bf16[512,512]{1,0:T(8,128)(2,1)S(1)}, bf16[512,512]{1,0:T(8,128)(2,1)}, u32[]{:S(2)}) copy-start(bf16[512,512]{1,0:T(8,128)(2,1)} %copy-done.5) | copy-start | bytes 1572868
  90.7 22.2 %collective-permute-start.14 = (bf16[256,512]{1,0:T(8,128)(2,1)S(1)}, bf16[256,512]{1,0:T(8,128)(2,1)S(1)}, u32[]{:S(2)}, u32[]{:S(2)}) collective-permute-start(bf16[256,512]{1,0:T(8,128)(2,1)S(1)} %upper.2), channel_id=1, source_target_pairs={{128,0},{160,32},{192,64},{224,96},{129,1},{161,33},{193,65},{225,... | collective-permute-start | bytes 786440 | tf_op jit(solution)/shard_map/ppermute | solution.py:394
  93.4 7.4 %copy-start.10 = (bf16[512,512]{1,0:T(8,128)(2,1)}, bf16[512,512]{1,0:T(8,128)(2,1)S(1)}, u32[]{:S(2)}) copy-start(bf16[512,512]{1,0:T(8,128)(2,1)S(1)} %collective-permute-done.16.cross) | copy-start | bytes 1572868
  99.6 21.6 %collective-permute-start.17 = (bf16[256,512]{1,0:T(8,128)(2,1)}, bf16[256,512]{1,0:T(8,128)(2,1)}, u32[]{:S(2)}, u32[]{:S(2)}) collective-permute-start(bf16[256,512]{1,0:T(8,128)(2,1)} %upper.3), channel_id=1, source_target_pairs={{128,0},{160,32},{192,64},{224,96},{129,1},{161,33},{193,65},{225,... | collective-permute-start | bytes 786440 | tf_op jit(solution)/shard_map/ppermute | solution.py:394
  112.9 0.7 copy-start.14
  113.5 1.0 copy-start.9
  114.6 0.9 copy-start.15
  115.5 5.7 %copy-start.2 = (bf16[2,2,1,128,4096]{4,3,2,1,0:T(8,128)(2,1)S(1)}, bf16[2,2,1,128,4096]{4,3,2,1,0:T(8,128)(2,1)}, u32[]{:S(2)}) copy-start(bf16[2,2,1,128,4096]{4,3,2,1,0:T(8,128)(2,1)} %param.7) | copy-start | bytes 12582916
  121.2 2.9 %copy-start.7 = (bf16[512,512]{1,0:T(8,128)(2,1)S(1)}, bf16[512,512]{1,0:T(8,128)(2,1)}, u32[]{:S(2)}) copy-start(bf16[512,512]{1,0:T(8,128)(2,1)} %copy-done.5) | copy-start | bytes 1572868
  121.2 2.9 %copy-start.11 = (bf16[512,512]{1,0:T(8,128)(2,1)S(1)}, bf16[512,512]{1,0:T(8,128)(2,1)}, u32[]{:S(2)}) copy-start(bf16[512,512]{1,0:T(8,128)(2,1)} %copy-done.10) | copy-start | bytes 1572868
  122.5 1.4 %collective-permute-start.18 = (f32[256,128]{1,0:T(8,128)S(1)}, f32[256,128]{1,0:T(8,128)S(1)}, u32[]{:S(2)}, u32[]{:S(2)}) collective-permute-start(f32[256,128]{1,0:T(8,128)S(1)} %rows_in.1), channel_id=1, source_target_pairs={{0,32},{32,0},{64,96},{96,64},{128,160},{160,128},{192,224},{224,1... | collective-permute-start | bytes 393224 | tf_op jit(solution)/shard_map/ppermute | solution.py:19
  124.0 8.4 %collective-permute-start.19 = (f32[2,256,128]{2,1,0:T(8,128)S(1)}, f32[2,256,128]{2,1,0:T(8,128)S(1)}, u32[]{:S(2)}, u32[]{:S(2)}) collective-permute-start(f32[2,256,128]{2,1,0:T(8,128)S(1)} %pad_maximum_fusion.2), channel_id=1, source_target_pairs={{0,64},{32,96},{64,0},{96,32},{128,192},{160,224},{192,128},{224,1... | collective-permute-start | bytes 786440 | tf_op jit(solution)/shard_map/ppermute | solution.py:19
  133.2 1.2 collective-permute-start.20
  134.5 6.0 %collective-permute-start.23 = (f32[64,128]{1,0:T(8,128)S(1)}, f32[64,128]{1,0:T(8,128)S(1)}, u32[]{:S(2)}, u32[]{:S(2)}) collective-permute-start(f32[64,128]{1,0:T(8,128)S(1)} %add.191), channel_id=1, source_target_pairs={{0,192},{32,224},{64,128},{96,160},{128,64},{160,96},{192,0},{224,... | collective-permute-start | bytes 98312 | tf_op jit(solution)/shard_map/ppermute | solution.py:19
  134.5 6.0 %collective-permute-start.22 = (f32[64,128]{1,0:T(8,128)S(1)}, f32[64,128]{1,0:T(8,128)S(1)}, u32[]{:S(2)}, u32[]{:S(2)}) collective-permute-start(f32[64,128]{1,0:T(8,128)S(1)} %add.191), channel_id=1, source_target_pairs={{0,128},{32,160},{64,192},{96,224},{128,0},{160,32},{192,64},{224,... | collective-permute-start | bytes 98312 | tf_op jit(solution)/shard_map/ppermute | solution.py:19
  136.3 4.6 %collective-permute-start.21 = (f32[64,128]{1,0:T(8,128)S(1)}, f32[64,128]{1,0:T(8,128)S(1)}, u32[]{:S(2)}, u32[]{:S(2)}) collective-permute-start(f32[64,128]{1,0:T(8,128)S(1)} %add.191), channel_id=1, source_target_pairs={{0,64},{32,96},{64,0},{96,32},{128,192},{160,224},{192,128},{224,1... | collective-permute-start | bytes 98312 | tf_op jit(solution)/shard_map/ppermute | solution.py:19

commit v2 on v1

--- a/solution.py
+++ b/solution.py
@@ -10,7 +10,7 @@
 F32 = jnp.float32
 CHUNKS = 2
 PIECES = ((0, 512), (512, 512))
-VMEM = 16 * 1024 * 1024
+VMEM = 8 * 1024 * 1024
 PARAMS = dict(compiler_params=pltpu.CompilerParams(vmem_limit_bytes=VMEM))
 
 
@@ -248,10 +248,14 @@
     )(place, cot, received, *gate_set, filt, gathered)
 
 
-def rows_in_body(acts_ref, basis_ref, out_ref):
+def rows_in_body(stored_ref, basis_ref, out_ref, acts_ref, done):
+    copies = [pltpu.make_async_copy(stored_ref.at[layer], acts_ref.at[layer], done.at[layer]) for layer in range(2)]
+    for copy in copies:
+        copy.start()
     lane = lax.broadcasted_iota(jnp.int32, (256, 128), 1)
     made = []
     for layer in range(2):
+        copies[layer].wait()
         total = jnp.zeros((256, 128), F32)
         for block in range(16):
             left = acts_ref[layer, :, block * 128 : block * 128 + 128]
@@ -265,16 +269,17 @@
 def project_in(acts, gathered):
     return pl.pallas_call(
         rows_in_body,
-        in_specs=held(2),
+        in_specs=[pl.BlockSpec(memory_space=pltpu.HBM)] + held(1),
         out_specs=held(1)[0],
         out_shape=jax.ShapeDtypeStruct((256, 128), F32),
+        scratch_shapes=[pltpu.VMEM((2, 256, 4096), BF), pltpu.SemaphoreType.DMA((2,))],
         name="rows_in",
         **PARAMS,
     )(acts, gathered)
 
 
 def term_body(*refs):
-    parts, rows_in_ref, out_ref = refs[:-2], refs[-2], refs[-1]
+    parts, rows_in, out_ref = refs[:-5], refs[-5:-1], refs[-1]
     for micro in range(2):
         rows = slice(micro * 128, micro * 128 + 128)
         total = jnp.zeros((128, 128), F32)
@@ -284,7 +289,7 @@
                 rows_out = rows_out + part[slot, rows, :]
             total = total + lax.dot_general(
                 rows_out,
-                rows_in_ref[slot, rows, :],
+                rows_in[slot][rows, :].astype(F32),
                 (((0,), (0,)), ((), ())),
                 preferred_element_type=F32,
                 precision=lax.Precision.HIGHEST,
@@ -295,12 +300,12 @@
 def terms(parts, rows_in):
     return pl.pallas_call(
         term_body,
-        in_specs=held(len(parts) + 1),
+        in_specs=held(len(parts) + 4),
         out_specs=held(1)[0],
         out_shape=jax.ShapeDtypeStruct((64, 128), F32),
         name="terms",
         **PARAMS,
-    )(*parts, rows_in)
+    )(*parts, *rows_in)
 
 
 def with_other(value):
@@ -387,19 +392,18 @@
     top = top_cotangent(dlogits, first)
 
     width = 1024 // CHUNKS
-    received = []
-    for chunk in range(CHUNKS):
-        start = after(top, passed) if chunk else top
-        passed = upper(chunk, width, place, start, gate_sets[piece_of(chunk)], filt)
-        received.append(lax.ppermute(passed, "section", [(s, s - 4) for s in range(4, 8)]))
-
-    start = after(received[0], passed)
-    parts = [lower(0, width, place, top, start, gate_sets[0], filt, second)]
-    rows_in = project_in(acts.reshape(2, 256, 4096), after(second, parts[0], received[1]))
-    start = after(received[1], rows_in)
+    passed = upper(0, width, place, top, gate_sets[0], filt)
+    down = [(s, s - 4) for s in range(4, 8)]
+    received = [lax.ppermute(passed, "section", down)]
+    rows_in = project_in(acts.reshape(2, 256, 4096), after(second, passed))
+    passed = upper(1, width, place, after(top, rows_in), gate_sets[1], filt)
+    received.append(lax.ppermute(passed, "section", down))
+    sent = rows_in.astype(BF)
+    rows_in = [rows_in] + [swap(sent, "section", bit) for bit in (1, 2, 3)]
+
+    parts = [lower(0, width, place, top, after(received[0], passed), gate_sets[0], filt, second)]
+    start = after(received[1], parts[0])
     parts.append(lower(1, width, place, top, start, gate_sets[1], filt, second))
-    rows_in = jnp.stack([rows_in, swap(rows_in, "section", 1)])
-    rows_in = jnp.concatenate([rows_in, swap(rows_in, "section", 2)], axis=0)
     feats = terms(parts, rows_in)
     feats = feats + swap(feats, "section", 1)
     feats = (feats + swap(feats, "section", 2)) + (swap(feats, "section", 4) + swap(feats, "section", 6))

time: 144 us -> 138 us (0.958)
  waiting for transfers between devices: 49.9 us -> 38.8 us
  starting transfers between devices: 45.1 us -> 50.4 us
    ppermute x2, waiting for transfers between devices: 12 us -> 5.29 us  [the longest x1 5.29 us: shards(): received.append(lax.ppermute(passed, 'section', down))]
    ppermute x21 -> x22, waiting for transfers between devices: 26.4 us -> 20.6 us  [swap(): return lax.ppermute(value, axis, [(i, i ^ bit) for i in range(count)])]
    ppermute x21 -> x22, starting transfers between devices: 27.1 us -> 32.4 us  [swap(): return lax.ppermute(value, axis, [(i, i ^ bit) for i in range(count)])]
    unnamed x42 -> x30, local copies, waits for them, and re-layouts: 3.53 us -> 3.03 us
  transfers between devices with their start and end apart: 26 -> 27, of which waited for: 14 -> 12; matrix products, arithmetic and copies ran while one was open for 4% -> 4% of each run, Pallas kernels for 19% -> 21%
where the time goes in v2:
time: 138 us; the launch traced here: 136 us
  starting transfers between devices  50.4 us (37%)
  waiting for transfers between devices  38.8 us (28%)
  Pallas kernels  34.8 us (25%)
  local copies, waits for them, and re-layouts  7.24 us (5%)
  other arithmetic  4.09 us (3%)
    ppermute x22, starting transfers between devices, swap(): return lax.ppermute(value, axis, [(i, i ^ bit) for i in range(count)])  32.4 us
    ppermute x22, waiting for transfers between devices, swap(): return lax.ppermute(value, axis, [(i, i ^ bit) for i in range(count)])  20.6 us
    all_to_all x2, waiting for transfers between devices, gather_xy(): out = lax.all_to_all(spread, 'dp', 0, 0, axis_index_groups=groups)  12.9 us
    pallas_call x2, Pallas kernels, upper(): pl.pallas_call(functools.partial(upper_body, chunk, width), in_specs=[pl....  11.8 us
    pallas_call x2, Pallas kernels, lower(): pl.pallas_call(functools.partial(lower_body, chunk, width), in_specs=[pl....  11 us
    all_to_all x2, starting transfers between devices, gather_xy(): out = lax.all_to_all(spread, 'dp', 0, 0, axis_index_groups=groups)  10.4 us
    pallas_call x1, Pallas kernels, sort_gates(): pl.pallas_call(gates_body, grid=(2,), in_specs=[pl.BlockSpec((256, 4096),...  5.67 us
    ppermute x1, waiting for transfers between devices, shards(): received.append(lax.ppermute(passed, 'section', down))  5.29 us
  transfers between devices with their start and end apart: 27, of which 12 were waited for; matrix products, arithmetic and copies ran while one was open for 4% of the time, Pallas kernels for 21%

profile of v2, /device:TPU:0, one launch (start us, length us, event | category | flops | bytes accessed | tf_op | source)
XLA Modules:
  0.0 135.9 jit_solution(18029015596442039965)
XLA Ops:
  0.2 0.9 pad_maximum_fusion.sort_ref
  1.1 5.7 %sort_gates.1 = (bf16[512,512]{1,0:T(8,128)(2,1)}, bf16[512,512]{1,0:T(8,128)(2,1)}, bf16[512,512]{1,0:T(8,128)(2,1)}, bf16[512,512]{1,0:T(8,128)(2,1)}, bf16[51...) custom-call(bf16[512,4096]{1,0:T(8,128)(2,1)} %bitcast.56, ...), custom_call_target="tpu_custom_call" | custom-call | tf_op jit(solution)/shard_map/sort_gates/pallas_call | solution.py:59
  6.8 0.5 collective-permute-start.5
  7.9 5.0 %collective-permute-start = (bf16[128,128]{1,0:T(8,128)(2,1)S(1)}, bf16[128,128]{1,0:T(8,128)(2,1)S(1)}, u32[]{:S(2)}, u32[]{:S(2)}) collective-permute-start(bf16[128,128]{1,0:T(8,128)(2,1)S(1)} %bitcast.69), channel_id=1, source_target_pairs={{0,208},{1,209},{2,210},{3,211},{4,212},{5,213},{6,214},{7,215},{8... | collective-permute-start | bytes 98312 | tf_op jit(solution)/shard_map/ppermute | solution.py:346
  12.9 0.7 pick_hidden.1.hidden_ref
  13.6 0.8 copy-done.8
  14.5 2.0 %collective-permute-start.2 = (bf16[2,36,128]{2,1,0:T(8,128)(2,1)S(1)}, bf16[2,36,128]{2,1,0:T(8,128)(2,1)S(1)}, u32[]{:S(2)}, u32[]{:S(2)}) collective-permute-start(bf16[2,36,128]{2,1,0:T(8,128)(2,1)S(1)} %get-tuple-element.68), channel_id=1, source_target_pairs={{0,64},{32,96},{64,0},{96,32},{128,192},{160,224},{192,128},{224,1... | collective-permute-start | bytes 55304 | tf_op jit(solution)/shard_map/ppermute | solution.py:19
  16.5 6.0 %collective-permute-done.2 = bf16[2,36,128]{2,1,0:T(8,128)(2,1)S(1)} collective-permute-done((bf16[2,36,128]{2,1,0:T(8,128)(2,1)S(1)}, bf16[2,36,128]{2,1,0:T(8,128)(2,1)S(1)}, u32[]{:S(2)}, u32[]{:S(2)}) %collective-permute-start.2) | collective-permute-done | bytes 18464 | tf_op jit(solution)/shard_map/ppermute | solution.py:19
  22.7 5.5 %collective-permute-start.3 = (bf16[272,128]{1,0:T(8,128)(2,1)S(1)}, bf16[272,128]{1,0:T(8,128)(2,1)S(1)}, u32[]{:S(2)}, u32[]{:S(2)}) collective-permute-start(bf16[272,128]{1,0:T(8,128)(2,1)S(1)} %pad_maximum_fusion.2), channel_id=1, source_target_pairs={{0,16},{1,17},{2,18},{3,19},{4,20},{5,21},{6,22},{7,23},{8,24},{9,... | collective-permute-start | bytes 208904 | tf_op jit(solution)/shard_map/ppermute | solution.py:19
  28.3 2.7 %collective-permute-done.3 = bf16[272,128]{1,0:T(8,128)(2,1)S(1)} collective-permute-done((bf16[272,128]{1,0:T(8,128)(2,1)S(1)}, bf16[272,128]{1,0:T(8,128)(2,1)S(1)}, u32[]{:S(2)}, u32[]{:S(2)}) %collective-permute-start.3) | collective-permute-done | bytes 69664 | tf_op jit(solution)/shard_map/ppermute | solution.py:19
  31.1 1.2 broadcast_in_dim.4
  32.3 6.6 %all-to-all-start = ((bf16[16,2,144,128]{3,2,1,0:T(8,128)(2,1)}), bf16[16,2,144,128]{3,2,1,0:T(8,128)(2,1)S(1)}, u32[]{:S(2)}, u32[]{:S(2)}) async-start(bf16[16,2,144,128]{3,2,1,0:T(8,128)(2,1)} %broadcast_in_dim.4), calls=%async_computation | async-start | bytes 2359296 | tf_op jit(solution)/shard_map/all_to_all | solution.py:320
  38.9 5.4 %collective-permute-start.8 = (bf16[512,512]{1,0:T(8,128)(2,1)}, bf16[512,512]{1,0:T(8,128)(2,1)}, u32[]{:S(2)}, u32[]{:S(2)}) collective-permute-start(bf16[512,512]{1,0:T(8,128)(2,1)} %get-tuple-element.48), channel_id=1, source_target_pairs={{0,64},{32,96},{64,0},{96,32},{128,192},{160,224},{192,128},{224,1... | collective-permute-start | bytes 1572872 | tf_op jit(solution)/shard_map/ppermute | solution.py:19
  44.4 11.5 %all-to-all-done = bf16[16,2,144,128]{3,2,1,0:T(8,128)(2,1)S(1)} async-done(((bf16[16,2,144,128]{3,2,1,0:T(8,128)(2,1)}), bf16[16,2,144,128]{3,2,1,0:T(8,128)(2,1)S(1)}, u32[]{:S(2)}, u32[]{:S(2)}) %all-to-all-start) | async-done | bytes 1179680 | tf_op jit(solution)/shard_map/all_to_all | solution.py:320
  56.0 1.7 %partial_logits.1 = (f32[128,512]{1,0:T(8,128)S(1)}, f32[128,512]{1,0:T(8,128)}) custom-call(s32[4]{0:T(128)S(1)} %pad_add_fusion.place_ref, bf16[256,1024]{1,0:T(8,128)(2,1)S(1)} %copy-done.9, bf16[32,144,128]{2,1,0:T(8,128)(2,1)S(1)} %bitcast.47), custom_call_target="tpu_custom_call" | custom-call | tf_op jit(solution)/shard_map/partial_logits/pallas_call | solution.py:108
  57.7 1.8 %broadcast_in_dim.5 = bf16[16,2,256,128]{3,2,1,0:T(8,128)(2,1)} broadcast(bf16[2,256,128]{2,1,0:T(8,128)(2,1)S(1)} %slice.35), dimensions={1,2,3} | broadcast | bytes 2228224 | tf_op jit(solution)/shard_map/broadcast_in_dim | solution.py:319
  59.5 3.8 %all-to-all-start.1 = ((bf16[16,2,256,128]{3,2,1,0:T(8,128)(2,1)}), bf16[16,2,256,128]{3,2,1,0:T(8,128)(2,1)S(1)}, u32[]{:S(2)}, u32[]{:S(2)}) async-start(bf16[16,2,256,128]{3,2,1,0:T(8,128)(2,1)} %broadcast_in_dim.5), calls=%async_computation.1 | async-start | bytes 4194304 | tf_op jit(solution)/shard_map/all_to_all | solution.py:320
  63.4 1.0 add.185
  64.4 1.6 %collective-permute-done.9.cross = bf16[512,512]{1,0:T(8,128)(2,1)} collective-permute-done((bf16[512,512]{1,0:T(8,128)(2,1)}, bf16[512,512]{1,0:T(8,128)(2,1)}, u32[]{:S(2)}, u32[]{:S(2)}) %collective-permute-start.9) | collective-permute-done | bytes 524320 | tf_op jit(solution)/shard_map/ppermute | solution.py:19
  66.0 4.5 %collective-permute-start.10 = (f32[64,512]{1,0:T(8,128)S(1)}, f32[64,512]{1,0:T(8,128)S(1)}, u32[]{:S(2)}, u32[]{:S(2)}) collective-permute-start(f32[64,512]{1,0:T(8,128)S(1)} %constant_dynamic-slice_fusion), channel_id=1, source_target_pairs={{0,64},{32,96},{64,0},{96,32},{128,192},{160,224},{192,128},{224,1... | collective-permute-start | bytes 393224 | tf_op jit(solution)/shard_map/ppermute | solution.py:19
  70.5 0.2 collective-permute-start.13
  70.7 0.3 collective-permute-start.15
  71.1 3.6 %collective-permute-done.10 = f32[64,512]{1,0:T(8,128)S(1)} collective-permute-done((f32[64,512]{1,0:T(8,128)S(1)}, f32[64,512]{1,0:T(8,128)S(1)}, u32[]{:S(2)}, u32[]{:S(2)}) %collective-permute-start.10) | collective-permute-done | bytes 131104 | tf_op jit(solution)/shard_map/ppermute | solution.py:19
  74.6 1.0 fusion.18
  76.0 1.8 %collective-permute-start.11 = (bf16[64,512]{1,0:T(8,128)(2,1)S(1)}, bf16[64,512]{1,0:T(8,128)(2,1)S(1)}, u32[]{:S(2)}, u32[]{:S(2)}) collective-permute-start(bf16[64,512]{1,0:T(8,128)(2,1)S(1)} %subtract_convert_fusion), channel_id=1, source_target_pairs={{0,64},{32,96},{64,0},{96,32},{128,192},{160,224},{192,128},{224,1... | collective-permute-start | bytes 196616 | tf_op jit(solution)/shard_map/ppermute | solution.py:19
  78.0 2.4 %collective-permute-done.11 = bf16[64,512]{1,0:T(8,128)(2,1)S(1)} collective-permute-done((bf16[64,512]{1,0:T(8,128)(2,1)S(1)}, bf16[64,512]{1,0:T(8,128)(2,1)S(1)}, u32[]{:S(2)}, u32[]{:S(2)}) %collective-permute-start.11) | collective-permute-done | bytes 65568 | tf_op jit(solution)/shard_map/ppermute | solution.py:19
  80.3 1.7 %collective-permute-start.16 = (bf16[512,512]{1,0:T(8,128)(2,1)}, bf16[512,512]{1,0:T(8,128)(2,1)}, u32[]{:S(2)}, u32[]{:S(2)}) collective-permute-start(bf16[512,512]{1,0:T(8,128)(2,1)} %collective-permute-done.5), channel_id=1, source_target_pairs={{0,64},{32,96},{64,0},{96,32},{128,192},{160,224},{192,128},{224,1... | collective-permute-start | bytes 1572872 | tf_op jit(solution)/shard_map/ppermute | solution.py:19
  82.4 1.2 collective-permute-done.12
  83.7 1.4 %top_cotangent.1.cot_ref.top_ref = bf16[256,1024]{1,0:T(8,128)(2,1)S(1)} custom-call(bf16[256,512]{1,0:T(8,128)(2,1)S(1)} %maximum_select_fusion.dlogits_ref, bf16[32,144,128]{2,1,0:T(8,128)(2,1)S(1)} %bitcast.49), custom_call_target="tpu_custom_call" | custom-call | tf_op jit(solution)/shard_map/top_cotangent/pallas_call | solution.py:130
  85.1 6.3 %upper.2 = bf16[256,512]{1,0:T(8,128)(2,1)} custom-call(s32[4]{0:T(128)S(1)} %pad_add_fusion.place_ref, bf16[256,1024]{1,0:T(8,128)(2,1)S(1)} %top_cotangent.1.cot_ref.top_ref, bf16[512,512]{1,0:T(8,128)(2,1)S(1)} %copy-done.5, bf16[512,512]{1,0:T(8,128)(2,1)} %collective-permute-done.13.side, bf16[512,512]{1,0:T(8,128)(2,1)} %collective-permute-done.8.over, ...), custom_call_target="tpu_custom_call" | custom-call | tf_op jit(solution)/shard_map/upper/pallas_call | solution.py:229
  91.4 1.3 collective-permute-start.14
  92.7 1.4 %all-to-all-done.1 = bf16[16,2,256,128]{3,2,1,0:T(8,128)(2,1)S(1)} async-done(((bf16[16,2,256,128]{3,2,1,0:T(8,128)(2,1)}), bf16[16,2,256,128]{3,2,1,0:T(8,128)(2,1)S(1)}, u32[]{:S(2)}, u32[]{:S(2)}) %all-to-all-start.1) | async-done | bytes 2097184 | tf_op jit(solution)/shard_map/all_to_all | solution.py:320
  94.1 2.2 %copy-done.2 = bf16[2,2,1,128,4096]{4,3,2,1,0:T(8,128)(2,1)S(1)} copy-done((bf16[2,2,1,128,4096]{4,3,2,1,0:T(8,128)(2,1)S(1)}, bf16[2,2,1,128,4096]{4,3,2,1,0:T(8,128)(2,1)}, u32[]{:S(2)}) %copy-start.2) | copy-done | bytes 4194328
  96.3 1.7 %rows_in.1.refs_2_ = f32[256,128]{1,0:T(8,128)S(1)} custom-call(bf16[2,256,4096]{2,1,0:T(8,128)(2,1)S(1)} %bitcast.54, bf16[32,256,128]{2,1,0:T(8,128)(2,1)S(1)} %bitcast.44), custom_call_target="tpu_custom_call" | custom-call | tf_op jit(solution)/shard_map/rows_in/pallas_call | solution.py:270
  98.1 5.5 %upper.3 = bf16[256,512]{1,0:T(8,128)(2,1)S(1)} custom-call(s32[4]{0:T(128)S(1)} %pad_add_fusion.place_ref, bf16[256,1024]{1,0:T(8,128)(2,1)S(1)} %top_cotangent.1.cot_ref.top_ref, bf16[512,512]{1,0:T(8,128)(2,1)S(1)} %copy-done.4, bf16[512,512]{1,0:T(8,128)(2,1)} %collective-permute-done.15.side, bf16[512,512]{1,0:T(8,128)(2,1)S(1)} %copy-done.7, ...), custom_call_target="tpu_custom_call" | custom-call | tf_op jit(solution)/shard_map/upper/pallas_call | solution.py:229
  103.5 1.3 collective-permute-start.17
  104.9 4.2 %collective-permute-start.20 = (bf16[256,128]{1,0:T(8,128)(2,1)S(1)}, bf16[256,128]{1,0:T(8,128)(2,1)S(1)}, u32[]{:S(2)}, u32[]{:S(2)}) collective-permute-start(bf16[256,128]{1,0:T(8,128)(2,1)S(1)} %convert_element_type.29), channel_id=1, source_target_pairs={{0,96},{32,64},{64,32},{96,0},{128,224},{160,192},{192,160},{224,1... | collective-permute-start | bytes 196616 | tf_op jit(solution)/shard_map/ppermute | solution.py:19
  109.0 1.3 collective-permute-start.19
  110.4 5.6 %lower.2.refs_0_ = f32[4,256,128]{2,1,0:T(8,128)S(1)} custom-call(s32[4]{0:T(128)S(1)} %pad_add_fusion.place_ref, bf16[256,1024]{1,0:T(8,128)(2,1)S(1)} %top_cotangent.1.cot_ref.top_ref, bf16[256,512]{1,0:T(8,128)(2,1)} %collective-permute-done.14.recv_ref, bf16[512,512]{1,0:T(8,128)(2,1)S(1)} %copy-done.5, bf16[512,512]{1,0:T(8,128)(2,1)} %collective-permute-done.13.side, ...), custom_call_target="tpu_custom_call" | custom-call | tf_op jit(solution)/shard_map/lower/pallas_call | solution.py:240
  116.0 5.3 %collective-permute-done.17.recv_ref = bf16[256,512]{1,0:T(8,128)(2,1)S(1)} collective-permute-done((bf16[256,512]{1,0:T(8,128)(2,1)S(1)}, bf16[256,512]{1,0:T(8,128)(2,1)S(1)}, u32[]{:S(2)}, u32[]{:S(2)}) %collective-permute-start.17) | collective-permute-done | bytes 262176 | tf_op jit(solution)/shard_map/ppermute | solution.py:400
  121.3 5.4 %lower.3.refs_1_ = f32[4,256,128]{2,1,0:T(8,128)S(1)} custom-call(s32[4]{0:T(128)S(1)} %pad_add_fusion.place_ref, bf16[256,1024]{1,0:T(8,128)(2,1)S(1)} %top_cotangent.1.cot_ref.top_ref, bf16[256,512]{1,0:T(8,128)(2,1)S(1)} %collective-permute-done.17.recv_ref, bf16[512,512]{1,0:T(8,128)(2,1)S(1)} %copy-done.4, ...), custom_call_target="tpu_custom_call" | custom-call | tf_op jit(solution)/shard_map/lower/pallas_call | solution.py:240
  126.7 0.8 terms.1
  127.5 1.2 collective-permute-done.21
  128.8 0.7 collective-permute-start.23
  129.4 3.7 %collective-permute-start.22 = (f32[64,128]{1,0:T(8,128)S(1)}, f32[64,128]{1,0:T(8,128)S(1)}, u32[]{:S(2)}, u32[]{:S(2)}) collective-permute-start(f32[64,128]{1,0:T(8,128)S(1)} %add.191), channel_id=1, source_target_pairs={{0,64},{32,96},{64,0},{96,32},{128,192},{160,224},{192,128},{224,1... | collective-permute-start | bytes 98312 | tf_op jit(solution)/shard_map/ppermute | solution.py:19
  133.1 1.6 %collective-permute-done.24 = f32[64,128]{1,0:T(8,128)S(1)} collective-permute-done((f32[64,128]{1,0:T(8,128)S(1)}, f32[64,128]{1,0:T(8,128)S(1)}, u32[]{:S(2)}, u32[]{:S(2)}) %collective-permute-start.24) | collective-permute-done | bytes 32800 | tf_op jit(solution)/shard_map/ppermute | solution.py:19
  134.7 0.3 collective-permute-done.22
  135.2 0.7 reshape.81
  (93 shorter events, 2.3 us)
Async XLA Ops:
  1.1 6.4 %copy-start.13 = (bf16[2,8,128]{2,1,0:T(8,128)(2,1)S(1)}, bf16[2,8,128]{2,1,0:T(8,128)(2,1)}, u32[]{:S(2)}) copy-start(bf16[2,8,128]{2,1,0:T(8,128)(2,1)} %param.9) | copy-start | bytes 12292
  1.1 6.4 %copy-start.11 = (bf16[2,128,128]{2,1,0:T(8,128)(2,1)S(1)}, bf16[2,128,128]{2,1,0:T(8,128)(2,1)}, u32[]{:S(2)}) copy-start(bf16[2,128,128]{2,1,0:T(8,128)(2,1)} %param.10) | copy-start | bytes 196612
  1.1 6.7 %copy-start.12 = (bf16[128,512]{1,0:T(8,128)(2,1)S(1)}, bf16[128,512]{1,0:T(8,128)(2,1)}, u32[]{:S(2)}) copy-start(bf16[128,512]{1,0:T(8,128)(2,1)} %param.12) | copy-start | bytes 393220
  1.1 11.8 %copy-start.3 = (bf16[2,1,128,4096]{3,2,1,0:T(8,128)(2,1)S(1)}, bf16[2,1,128,4096]{3,2,1,0:T(8,128)(2,1)}, u32[]{:S(2)}) copy-start(bf16[2,1,128,4096]{3,2,1,0:T(8,128)(2,1)} %param.11) | copy-start | bytes 6291460
  6.8 24.2 %collective-permute-start.4 = (bf16[512,512]{1,0:T(8,128)(2,1)}, bf16[512,512]{1,0:T(8,128)(2,1)}, u32[]{:S(2)}, u32[]{:S(2)}) collective-permute-start(bf16[512,512]{1,0:T(8,128)(2,1)} %get-tuple-element.38), channel_id=1, source_target_pairs={{0,32},{32,0},{64,96},{96,64},{128,160},{160,128},{192,224},{224,1... | collective-permute-start | bytes 1572872 | tf_op jit(solution)/shard_map/ppermute | solution.py:19
  6.8 24.2 %collective-permute-start.5 = (bf16[512,512]{1,0:T(8,128)(2,1)}, bf16[512,512]{1,0:T(8,128)(2,1)}, u32[]{:S(2)}, u32[]{:S(2)}) collective-permute-start(bf16[512,512]{1,0:T(8,128)(2,1)} %get-tuple-element.39), channel_id=1, source_target_pairs={{0,32},{32,0},{64,96},{96,64},{128,160},{160,128},{192,224},{224,1... | collective-permute-start | bytes 1572872 | tf_op jit(solution)/shard_map/ppermute | solution.py:19
  7.3 23.7 %collective-permute-start.6 = (bf16[512,512]{1,0:T(8,128)(2,1)}, bf16[512,512]{1,0:T(8,128)(2,1)S(1)}, u32[]{:S(2)}, u32[]{:S(2)}) collective-permute-start(bf16[512,512]{1,0:T(8,128)(2,1)} %get-tuple-element.35), channel_id=1, source_target_pairs={{0,64},{32,96},{64,0},{96,32},{128,192},{160,224},{192,128},{224,1... | collective-permute-start | bytes 1572872 | tf_op jit(solution)/shard_map/ppermute | solution.py:19
  7.7 6.8 %collective-permute-start.1 = (bf16[2,36,128]{2,1,0:T(8,128)(2,1)S(1)}, bf16[2,36,128]{2,1,0:T(8,128)(2,1)S(1)}, u32[]{:S(2)}, u32[]{:S(2)}) collective-permute-start(bf16[2,36,128]{2,1,0:T(8,128)(2,1)S(1)} %get-tuple-element.69), channel_id=1, source_target_pairs={{0,32},{32,0},{64,96},{96,64},{128,160},{160,128},{192,224},{224,1... | collective-permute-start | bytes 55304 | tf_op jit(solution)/shard_map/ppermute | solution.py:19
  7.9 8.6 %collective-permute-start = (bf16[128,128]{1,0:T(8,128)(2,1)S(1)}, bf16[128,128]{1,0:T(8,128)(2,1)S(1)}, u32[]{:S(2)}, u32[]{:S(2)}) collective-permute-start(bf16[128,128]{1,0:T(8,128)(2,1)S(1)} %bitcast.69), channel_id=1, source_target_pairs={{0,208},{1,209},{2,210},{3,211},{4,212},{5,213},{6,214},{7,215},{8... | collective-permute-start | bytes 98312 | tf_op jit(solution)/shard_map/ppermute | solution.py:346
  13.6 0.8 copy-start.8
  14.5 8.1 %collective-permute-start.2 = (bf16[2,36,128]{2,1,0:T(8,128)(2,1)S(1)}, bf16[2,36,128]{2,1,0:T(8,128)(2,1)S(1)}, u32[]{:S(2)}, u32[]{:S(2)}) collective-permute-start(bf16[2,36,128]{2,1,0:T(8,128)(2,1)S(1)} %get-tuple-element.68), channel_id=1, source_target_pairs={{0,64},{32,96},{64,0},{96,32},{128,192},{160,224},{192,128},{224,1... | collective-permute-start | bytes 55304 | tf_op jit(solution)/shard_map/ppermute | solution.py:19
  22.7 33.3 %copy-start.9 = (bf16[256,1024]{1,0:T(8,128)(2,1)S(1)}, bf16[256,1024]{1,0:T(8,128)(2,1)}, u32[]{:S(2)}) copy-start(bf16[256,1024]{1,0:T(8,128)(2,1)} %copy-done.8) | copy-start | bytes 1572868
  22.7 8.3 %collective-permute-start.3 = (bf16[272,128]{1,0:T(8,128)(2,1)S(1)}, bf16[272,128]{1,0:T(8,128)(2,1)S(1)}, u32[]{:S(2)}, u32[]{:S(2)}) collective-permute-start(bf16[272,128]{1,0:T(8,128)(2,1)S(1)} %pad_maximum_fusion.2), channel_id=1, source_target_pairs={{0,16},{1,17},{2,18},{3,19},{4,20},{5,21},{6,22},{7,23},{8,24},{9,... | collective-permute-start | bytes 208904 | tf_op jit(solution)/shard_map/ppermute | solution.py:19
  31.0 1.3 copy-start.6
  32.3 23.7 %all-to-all-start = ((bf16[16,2,144,128]{3,2,1,0:T(8,128)(2,1)}), bf16[16,2,144,128]{3,2,1,0:T(8,128)(2,1)S(1)}, u32[]{:S(2)}, u32[]{:S(2)}) async-start(bf16[16,2,144,128]{3,2,1,0:T(8,128)(2,1)} %broadcast_in_dim.4), calls=%async_computation | async-start | bytes 2359296 | tf_op jit(solution)/shard_map/all_to_all | solution.py:320
  38.9 25.5 %collective-permute-start.8 = (bf16[512,512]{1,0:T(8,128)(2,1)}, bf16[512,512]{1,0:T(8,128)(2,1)}, u32[]{:S(2)}, u32[]{:S(2)}) collective-permute-start(bf16[512,512]{1,0:T(8,128)(2,1)} %get-tuple-element.48), channel_id=1, source_target_pairs={{0,64},{32,96},{64,0},{96,32},{128,192},{160,224},{192,128},{224,1... | collective-permute-start | bytes 1572872 | tf_op jit(solution)/shard_map/ppermute | solution.py:19
  44.3 21.7 %collective-permute-start.9 = (bf16[512,512]{1,0:T(8,128)(2,1)}, bf16[512,512]{1,0:T(8,128)(2,1)}, u32[]{:S(2)}, u32[]{:S(2)}) collective-permute-start(bf16[512,512]{1,0:T(8,128)(2,1)} %collective-permute-done.4), channel_id=1, source_target_pairs={{0,64},{32,96},{64,0},{96,32},{128,192},{160,224},{192,128},{224,1... | collective-permute-start | bytes 1572872 | tf_op jit(solution)/shard_map/ppermute | solution.py:19
  55.9 21.9 %copy-start = (bf16[16,2,144,128]{3,2,1,0:T(8,128)(2,1)}, bf16[16,2,144,128]{3,2,1,0:T(8,128)(2,1)S(1)}, u32[]{:S(2)}) copy-start(bf16[16,2,144,128]{3,2,1,0:T(8,128)(2,1)S(1)} %all-to-all-done) | copy-start | bytes 3538948
  57.7 5.7 %collective-permute-start.7 = (f32[128,512]{1,0:T(8,128)}, f32[128,512]{1,0:T(8,128)}, u32[]{:S(2)}, u32[]{:S(2)}) collective-permute-start(f32[128,512]{1,0:T(8,128)} %get-tuple-element.47), channel_id=1, source_target_pairs={{0,32},{32,0},{64,96},{96,64},{128,160},{160,128},{192,224},{224,1... | collective-permute-start | bytes 786440 | tf_op jit(solution)/shard_map/ppermute | solution.py:19
  59.5 11.5 %copy-start.14 = (s32[2,1,128]{2,1,0:T(1,128)S(1)}, s32[2,1,128]{2,1,0:T(1,128)}, u32[]{:S(2)}) copy-start(s32[2,1,128]{2,1,0:T(1,128)} %param.13) | copy-start | bytes 3076
  59.5 34.6 %all-to-all-start.1 = ((bf16[16,2,256,128]{3,2,1,0:T(8,128)(2,1)}), bf16[16,2,256,128]{3,2,1,0:T(8,128)(2,1)S(1)}, u32[]{:S(2)}, u32[]{:S(2)}) async-start(bf16[16,2,256,128]{3,2,1,0:T(8,128)(2,1)} %broadcast_in_dim.5), calls=%async_computation.1 | async-start | bytes 4194304 | tf_op jit(solution)/shard_map/all_to_all | solution.py:320
  64.4 1.6 %copy-start.10 = (f32[128,512]{1,0:T(8,128)}, f32[128,512]{1,0:T(8,128)S(1)}, u32[]{:S(2)}) copy-start(f32[128,512]{1,0:T(8,128)S(1)} %add.185) | copy-start | bytes 786436
  66.0 8.6 %collective-permute-start.10 = (f32[64,512]{1,0:T(8,128)S(1)}, f32[64,512]{1,0:T(8,128)S(1)}, u32[]{:S(2)}, u32[]{:S(2)}) collective-permute-start(f32[64,512]{1,0:T(8,128)S(1)} %constant_dynamic-slice_fusion), channel_id=1, source_target_pairs={{0,64},{32,96},{64,0},{96,32},{128,192},{160,224},{192,128},{224,1... | collective-permute-start | bytes 393224 | tf_op jit(solution)/shard_map/ppermute | solution.py:19
  70.5 14.7 %collective-permute-start.13 = (bf16[512,512]{1,0:T(8,128)(2,1)}, bf16[512,512]{1,0:T(8,128)(2,1)}, u32[]{:S(2)}, u32[]{:S(2)}) collective-permute-start(bf16[512,512]{1,0:T(8,128)(2,1)} %get-tuple-element.36), channel_id=1, source_target_pairs={{0,32},{32,0},{64,96},{96,64},{128,160},{160,128},{192,224},{224,1... | collective-permute-start | bytes 1572872 | tf_op jit(solution)/shard_map/ppermute | solution.py:19
  70.7 27.3 %collective-permute-start.15 = (bf16[512,512]{1,0:T(8,128)(2,1)}, bf16[512,512]{1,0:T(8,128)(2,1)}, u32[]{:S(2)}, u32[]{:S(2)}) collective-permute-start(bf16[512,512]{1,0:T(8,128)(2,1)} %get-tuple-element.37), channel_id=1, source_target_pairs={{0,32},{32,0},{64,96},{96,64},{128,160},{160,128},{192,224},{224,1... | collective-permute-start | bytes 1572872 | tf_op jit(solution)/shard_map/ppermute | solution.py:19
  76.0 4.4 %collective-permute-start.11 = (bf16[64,512]{1,0:T(8,128)(2,1)S(1)}, bf16[64,512]{1,0:T(8,128)(2,1)S(1)}, u32[]{:S(2)}, u32[]{:S(2)}) collective-permute-start(bf16[64,512]{1,0:T(8,128)(2,1)S(1)} %subtract_convert_fusion), channel_id=1, source_target_pairs={{0,64},{32,96},{64,0},{96,32},{128,192},{160,224},{192,128},{224,1... | collective-permute-start | bytes 196616 | tf_op jit(solution)/shard_map/ppermute | solution.py:19
  77.8 5.9 %copy-start.1 = (bf16[16,2,144,128]{3,2,1,0:T(8,128)(2,1)S(1)}, bf16[16,2,144,128]{3,2,1,0:T(8,128)(2,1)}, u32[]{:S(2)}) copy-start(bf16[16,2,144,128]{3,2,1,0:T(8,128)(2,1)} %copy-done) | copy-start | bytes 3538948
  77.9 7.3 %copy-start.5 = (bf16[512,512]{1,0:T(8,128)(2,1)S(1)}, bf16[512,512]{1,0:T(8,128)(2,1)}, u32[]{:S(2)}) copy-start(bf16[512,512]{1,0:T(8,128)(2,1)} %get-tuple-element.32.near) | copy-start | bytes 1572868
  80.3 17.7 %collective-permute-start.16 = (bf16[512,512]{1,0:T(8,128)(2,1)}, bf16[512,512]{1,0:T(8,128)(2,1)}, u32[]{:S(2)}, u32[]{:S(2)}) collective-permute-start(bf16[512,512]{1,0:T(8,128)(2,1)} %collective-permute-done.5), channel_id=1, source_target_pairs={{0,64},{32,96},{64,0},{96,32},{128,192},{160,224},{192,128},{224,1... | collective-permute-start | bytes 1572872 | tf_op jit(solution)/shard_map/ppermute | solution.py:19
  82.2 1.4 %collective-permute-start.12 = (bf16[128,512]{1,0:T(8,128)(2,1)S(1)}, bf16[128,512]{1,0:T(8,128)(2,1)S(1)}, u32[]{:S(2)}, u32[]{:S(2)}) collective-permute-start(bf16[128,512]{1,0:T(8,128)(2,1)S(1)} %maximum_select_fusion.2), channel_id=1, source_target_pairs={{0,32},{32,0},{64,96},{96,64},{128,160},{160,128},{192,224},{224,1... | collective-permute-start | bytes 393224 | tf_op jit(solution)/shard_map/ppermute | solution.py:19
  91.4 18.9 %collective-permute-start.14 = (bf16[256,512]{1,0:T(8,128)(2,1)}, bf16[256,512]{1,0:T(8,128)(2,1)}, u32[]{:S(2)}, u32[]{:S(2)}) collective-permute-start(bf16[256,512]{1,0:T(8,128)(2,1)} %upper.2), channel_id=1, source_target_pairs={{128,0},{160,32},{192,64},{224,96},{129,1},{161,33},{193,65},{225,... | collective-permute-start | bytes 786440 | tf_op jit(solution)/shard_map/ppermute | solution.py:397
  94.1 2.2 %copy-start.2 = (bf16[2,2,1,128,4096]{4,3,2,1,0:T(8,128)(2,1)S(1)}, bf16[2,2,1,128,4096]{4,3,2,1,0:T(8,128)(2,1)}, u32[]{:S(2)}) copy-start(bf16[2,2,1,128,4096]{4,3,2,1,0:T(8,128)(2,1)} %param.7) | copy-start | bytes 12582916
  96.3 1.8 %copy-start.4 = (bf16[512,512]{1,0:T(8,128)(2,1)S(1)}, bf16[512,512]{1,0:T(8,128)(2,1)}, u32[]{:S(2)}) copy-start(bf16[512,512]{1,0:T(8,128)(2,1)} %get-tuple-element.33.near) | copy-start | bytes 1572868
  96.3 1.8 %copy-start.7 = (bf16[512,512]{1,0:T(8,128)(2,1)S(1)}, bf16[512,512]{1,0:T(8,128)(2,1)}, u32[]{:S(2)}) copy-start(bf16[512,512]{1,0:T(8,128)(2,1)} %copy-done.6) | copy-start | bytes 1572868
  103.5 17.7 %collective-permute-start.17 = (bf16[256,512]{1,0:T(8,128)(2,1)S(1)}, bf16[256,512]{1,0:T(8,128)(2,1)S(1)}, u32[]{:S(2)}, u32[]{:S(2)}) collective-permute-start(bf16[256,512]{1,0:T(8,128)(2,1)S(1)} %upper.3), channel_id=1, source_target_pairs={{128,0},{160,32},{192,64},{224,96},{129,1},{161,33},{193,65},{225,... | collective-permute-start | bytes 786440 | tf_op jit(solution)/shard_map/ppermute | solution.py:400
  104.9 21.8 %collective-permute-start.20 = (bf16[256,128]{1,0:T(8,128)(2,1)S(1)}, bf16[256,128]{1,0:T(8,128)(2,1)S(1)}, u32[]{:S(2)}, u32[]{:S(2)}) collective-permute-start(bf16[256,128]{1,0:T(8,128)(2,1)S(1)} %convert_element_type.29), channel_id=1, source_target_pairs={{0,96},{32,64},{64,32},{96,0},{128,224},{160,192},{192,160},{224,1... | collective-permute-start | bytes 196616 | tf_op jit(solution)/shard_map/ppermute | solution.py:19
  109.0 17.6 %collective-permute-start.19 = (bf16[256,128]{1,0:T(8,128)(2,1)S(1)}, bf16[256,128]{1,0:T(8,128)(2,1)S(1)}, u32[]{:S(2)}, u32[]{:S(2)}) collective-permute-start(bf16[256,128]{1,0:T(8,128)(2,1)S(1)} %convert_element_type.29), channel_id=1, source_target_pairs={{0,64},{32,96},{64,0},{96,32},{128,192},{160,224},{192,128},{224,1... | collective-permute-start | bytes 196616 | tf_op jit(solution)/shard_map/ppermute | solution.py:19
  110.3 16.3 %collective-permute-start.18 = (bf16[256,128]{1,0:T(8,128)(2,1)S(1)}, bf16[256,128]{1,0:T(8,128)(2,1)S(1)}, u32[]{:S(2)}, u32[]{:S(2)}) collective-permute-start(bf16[256,128]{1,0:T(8,128)(2,1)S(1)} %convert_element_type.29), channel_id=1, source_target_pairs={{0,32},{32,0},{64,96},{96,64},{128,160},{160,128},{192,224},{224,1... | collective-permute-start | bytes 196616 | tf_op jit(solution)/shard_map/ppermute | solution.py:19
  127.5 1.2 collective-permute-start.21
  128.7 6.0 %collective-permute-start.24 = (f32[64,128]{1,0:T(8,128)S(1)}, f32[64,128]{1,0:T(8,128)S(1)}, u32[]{:S(2)}, u32[]{:S(2)}) collective-permute-start(f32[64,128]{1,0:T(8,128)S(1)} %add.191), channel_id=1, source_target_pairs={{0,192},{32,224},{64,128},{96,160},{128,64},{160,96},{192,0},{224,... | collective-permute-start | bytes 98312 | tf_op jit(solution)/shard_map/ppermute | solution.py:19
  128.8 6.0 %collective-permute-start.23 = (f32[64,128]{1,0:T(8,128)S(1)}, f32[64,128]{1,0:T(8,128)S(1)}, u32[]{:S(2)}, u32[]{:S(2)}) collective-permute-start(f32[64,128]{1,0:T(8,128)S(1)} %add.191), channel_id=1, source_target_pairs={{0,128},{32,160},{64,192},{96,224},{128,0},{160,32},{192,64},{224,... | collective-permute-start | bytes 98312 | tf_op jit(solution)/shard_map/ppermute | solution.py:19
  129.4 5.6 %collective-permute-start.22 = (f32[64,128]{1,0:T(8,128)S(1)}, f32[64,128]{1,0:T(8,128)S(1)}, u32[]{:S(2)}, u32[]{:S(2)}) collective-permute-start(f32[64,128]{1,0:T(8,128)S(1)} %add.191), channel_id=1, source_target_pairs={{0,64},{32,96},{64,0},{96,32},{128,192},{160,224},{192,128},{224,1... | collective-permute-start | bytes 98312 | tf_op jit(solution)/shard_map/ppermute | solution.py:19

commit v3 on v2

--- a/solution.py
+++ b/solution.py
@@ -248,14 +248,10 @@
     )(place, cot, received, *gate_set, filt, gathered)
 
 
-def rows_in_body(stored_ref, basis_ref, out_ref, acts_ref, done):
-    copies = [pltpu.make_async_copy(stored_ref.at[layer], acts_ref.at[layer], done.at[layer]) for layer in range(2)]
-    for copy in copies:
-        copy.start()
+def rows_in_body(acts_ref, basis_ref, out_ref):
     lane = lax.broadcasted_iota(jnp.int32, (256, 128), 1)
     made = []
     for layer in range(2):
-        copies[layer].wait()
         total = jnp.zeros((256, 128), F32)
         for block in range(16):
             left = acts_ref[layer, :, block * 128 : block * 128 + 128]
@@ -269,10 +265,9 @@
 def project_in(acts, gathered):
     return pl.pallas_call(
         rows_in_body,
-        in_specs=[pl.BlockSpec(memory_space=pltpu.HBM)] + held(1),
+        in_specs=held(2),
         out_specs=held(1)[0],
         out_shape=jax.ShapeDtypeStruct((256, 128), F32),
-        scratch_shapes=[pltpu.VMEM((2, 256, 4096), BF), pltpu.SemaphoreType.DMA((2,))],
         name="rows_in",
         **PARAMS,
     )(acts, gathered)

time: 138 us -> 138 us (level)
  no operation moved by 1% of the time
where the time goes in v3:
time: 138 us; the launch traced here: 135 us
  starting transfers between devices  50.5 us (37%)
  waiting for transfers between devices  38.8 us (28%)
  Pallas kernels  34.3 us (25%)
  local copies, waits for them, and re-layouts  7.24 us (5%)
  other arithmetic  4.09 us (3%)
    ppermute x22, starting transfers between devices, swap(): return lax.ppermute(value, axis, [(i, i ^ bit) for i in range(count)])  32.4 us
    ppermute x22, waiting for transfers between devices, swap(): return lax.ppermute(value, axis, [(i, i ^ bit) for i in range(count)])  20.6 us
    all_to_all x2, waiting for transfers between devices, gather_xy(): out = lax.all_to_all(spread, 'dp', 0, 0, axis_index_groups=groups)  12.9 us
    pallas_call x2, Pallas kernels, upper(): pl.pallas_call(functools.partial(upper_body, chunk, width), in_specs=[pl....  11.8 us
    pallas_call x2, Pallas kernels, lower(): pl.pallas_call(functools.partial(lower_body, chunk, width), in_specs=[pl....  11 us
    all_to_all x2, starting transfers between devices, gather_xy(): out = lax.all_to_all(spread, 'dp', 0, 0, axis_index_groups=groups)  10.4 us
    pallas_call x1, Pallas kernels, sort_gates(): pl.pallas_call(gates_body, grid=(2,), in_specs=[pl.BlockSpec((256, 4096),...  5.67 us
    ppermute x1, waiting for transfers between devices, shards(): received.append(lax.ppermute(passed, 'section', down))  5.28 us
  transfers between devices with their start and end apart: 27, of which 12 were waited for; matrix products, arithmetic and copies ran while one was open for 4% of the time, Pallas kernels for 21%

profile of v3, /device:TPU:0, one launch (start us, length us, event | category | flops | bytes accessed | tf_op | source)
XLA Modules:
  0.0 135.4 jit_solution(16436287926490705193)
XLA Ops:
  0.2 0.9 pad_maximum_fusion.sort_ref
  1.1 5.7 %sort_gates.1 = (bf16[512,512]{1,0:T(8,128)(2,1)}, bf16[512,512]{1,0:T(8,128)(2,1)}, bf16[512,512]{1,0:T(8,128)(2,1)}, bf16[512,512]{1,0:T(8,128)(2,1)}, bf16[51...) custom-call(bf16[512,4096]{1,0:T(8,128)(2,1)} %bitcast.56, ...), custom_call_target="tpu_custom_call" | custom-call | tf_op jit(solution)/shard_map/sort_gates/pallas_call | solution.py:59
  6.8 0.5 collective-permute-start.5
  7.9 5.0 %collective-permute-start = (bf16[128,128]{1,0:T(8,128)(2,1)S(1)}, bf16[128,128]{1,0:T(8,128)(2,1)S(1)}, u32[]{:S(2)}, u32[]{:S(2)}) collective-permute-start(bf16[128,128]{1,0:T(8,128)(2,1)S(1)} %bitcast.69), channel_id=1, source_target_pairs={{0,208},{1,209},{2,210},{3,211},{4,212},{5,213},{6,214},{7,215},{8... | collective-permute-start | bytes 98312 | tf_op jit(solution)/shard_map/ppermute | solution.py:341
  12.9 0.7 pick_hidden.1.hidden_ref
  13.6 0.8 copy-done.8
  14.5 2.0 %collective-permute-start.2 = (bf16[2,36,128]{2,1,0:T(8,128)(2,1)S(1)}, bf16[2,36,128]{2,1,0:T(8,128)(2,1)S(1)}, u32[]{:S(2)}, u32[]{:S(2)}) collective-permute-start(bf16[2,36,128]{2,1,0:T(8,128)(2,1)S(1)} %get-tuple-element.68), channel_id=1, source_target_pairs={{0,64},{32,96},{64,0},{96,32},{128,192},{160,224},{192,128},{224,1... | collective-permute-start | bytes 55304 | tf_op jit(solution)/shard_map/ppermute | solution.py:19
  16.5 6.0 %collective-permute-done.2 = bf16[2,36,128]{2,1,0:T(8,128)(2,1)S(1)} collective-permute-done((bf16[2,36,128]{2,1,0:T(8,128)(2,1)S(1)}, bf16[2,36,128]{2,1,0:T(8,128)(2,1)S(1)}, u32[]{:S(2)}, u32[]{:S(2)}) %collective-permute-start.2) | collective-permute-done | bytes 18464 | tf_op jit(solution)/shard_map/ppermute | solution.py:19
  22.7 5.5 %collective-permute-start.3 = (bf16[272,128]{1,0:T(8,128)(2,1)S(1)}, bf16[272,128]{1,0:T(8,128)(2,1)S(1)}, u32[]{:S(2)}, u32[]{:S(2)}) collective-permute-start(bf16[272,128]{1,0:T(8,128)(2,1)S(1)} %pad_maximum_fusion.2), channel_id=1, source_target_pairs={{0,16},{1,17},{2,18},{3,19},{4,20},{5,21},{6,22},{7,23},{8,24},{9,... | collective-permute-start | bytes 208904 | tf_op jit(solution)/shard_map/ppermute | solution.py:19
  28.3 2.7 %collective-permute-done.3 = bf16[272,128]{1,0:T(8,128)(2,1)S(1)} collective-permute-done((bf16[272,128]{1,0:T(8,128)(2,1)S(1)}, bf16[272,128]{1,0:T(8,128)(2,1)S(1)}, u32[]{:S(2)}, u32[]{:S(2)}) %collective-permute-start.3) | collective-permute-done | bytes 69664 | tf_op jit(solution)/shard_map/ppermute | solution.py:19
  31.1 1.2 broadcast_in_dim.4
  32.3 6.6 %all-to-all-start = ((bf16[16,2,144,128]{3,2,1,0:T(8,128)(2,1)}), bf16[16,2,144,128]{3,2,1,0:T(8,128)(2,1)S(1)}, u32[]{:S(2)}, u32[]{:S(2)}) async-start(bf16[16,2,144,128]{3,2,1,0:T(8,128)(2,1)} %broadcast_in_dim.4), calls=%async_computation | async-start | bytes 2359296 | tf_op jit(solution)/shard_map/all_to_all | solution.py:315
  38.9 5.4 %collective-permute-start.8 = (bf16[512,512]{1,0:T(8,128)(2,1)}, bf16[512,512]{1,0:T(8,128)(2,1)}, u32[]{:S(2)}, u32[]{:S(2)}) collective-permute-start(bf16[512,512]{1,0:T(8,128)(2,1)} %get-tuple-element.48), channel_id=1, source_target_pairs={{0,64},{32,96},{64,0},{96,32},{128,192},{160,224},{192,128},{224,1... | collective-permute-start | bytes 1572872 | tf_op jit(solution)/shard_map/ppermute | solution.py:19
  44.4 11.5 %all-to-all-done = bf16[16,2,144,128]{3,2,1,0:T(8,128)(2,1)S(1)} async-done(((bf16[16,2,144,128]{3,2,1,0:T(8,128)(2,1)}), bf16[16,2,144,128]{3,2,1,0:T(8,128)(2,1)S(1)}, u32[]{:S(2)}, u32[]{:S(2)}) %all-to-all-start) | async-done | bytes 1179680 | tf_op jit(solution)/shard_map/all_to_all | solution.py:315
  56.0 1.7 %partial_logits.1 = (f32[128,512]{1,0:T(8,128)S(1)}, f32[128,512]{1,0:T(8,128)}) custom-call(s32[4]{0:T(128)S(1)} %pad_add_fusion.place_ref, bf16[256,1024]{1,0:T(8,128)(2,1)S(1)} %copy-done.9, bf16[32,144,128]{2,1,0:T(8,128)(2,1)S(1)} %bitcast.47), custom_call_target="tpu_custom_call" | custom-call | tf_op jit(solution)/shard_map/partial_logits/pallas_call | solution.py:108
  57.7 1.8 %broadcast_in_dim.5 = bf16[16,2,256,128]{3,2,1,0:T(8,128)(2,1)} broadcast(bf16[2,256,128]{2,1,0:T(8,128)(2,1)S(1)} %slice.35), dimensions={1,2,3} | broadcast | bytes 2228224 | tf_op jit(solution)/shard_map/broadcast_in_dim | solution.py:314
  59.5 3.8 %all-to-all-start.1 = ((bf16[16,2,256,128]{3,2,1,0:T(8,128)(2,1)}), bf16[16,2,256,128]{3,2,1,0:T(8,128)(2,1)S(1)}, u32[]{:S(2)}, u32[]{:S(2)}) async-start(bf16[16,2,256,128]{3,2,1,0:T(8,128)(2,1)} %broadcast_in_dim.5), calls=%async_computation.1 | async-start | bytes 4194304 | tf_op jit(solution)/shard_map/all_to_all | solution.py:315
  63.4 1.0 add.185
  64.4 1.6 %collective-permute-done.9.cross = bf16[512,512]{1,0:T(8,128)(2,1)} collective-permute-done((bf16[512,512]{1,0:T(8,128)(2,1)}, bf16[512,512]{1,0:T(8,128)(2,1)}, u32[]{:S(2)}, u32[]{:S(2)}) %collective-permute-start.9) | collective-permute-done | bytes 524320 | tf_op jit(solution)/shard_map/ppermute | solution.py:19
  66.0 4.5 %collective-permute-start.10 = (f32[64,512]{1,0:T(8,128)S(1)}, f32[64,512]{1,0:T(8,128)S(1)}, u32[]{:S(2)}, u32[]{:S(2)}) collective-permute-start(f32[64,512]{1,0:T(8,128)S(1)} %constant_dynamic-slice_fusion), channel_id=1, source_target_pairs={{0,64},{32,96},{64,0},{96,32},{128,192},{160,224},{192,128},{224,1... | collective-permute-start | bytes 393224 | tf_op jit(solution)/shard_map/ppermute | solution.py:19
  70.5 0.2 collective-permute-start.13
  70.7 0.3 collective-permute-start.15
  71.1 3.6 %collective-permute-done.10 = f32[64,512]{1,0:T(8,128)S(1)} collective-permute-done((f32[64,512]{1,0:T(8,128)S(1)}, f32[64,512]{1,0:T(8,128)S(1)}, u32[]{:S(2)}, u32[]{:S(2)}) %collective-permute-start.10) | collective-permute-done | bytes 131104 | tf_op jit(solution)/shard_map/ppermute | solution.py:19
  74.6 1.0 fusion.18
  76.0 1.8 %collective-permute-start.11 = (bf16[64,512]{1,0:T(8,128)(2,1)S(1)}, bf16[64,512]{1,0:T(8,128)(2,1)S(1)}, u32[]{:S(2)}, u32[]{:S(2)}) collective-permute-start(bf16[64,512]{1,0:T(8,128)(2,1)S(1)} %subtract_convert_fusion), channel_id=1, source_target_pairs={{0,64},{32,96},{64,0},{96,32},{128,192},{160,224},{192,128},{224,1... | collective-permute-start | bytes 196616 | tf_op jit(solution)/shard_map/ppermute | solution.py:19
  78.0 2.4 %collective-permute-done.11 = bf16[64,512]{1,0:T(8,128)(2,1)S(1)} collective-permute-done((bf16[64,512]{1,0:T(8,128)(2,1)S(1)}, bf16[64,512]{1,0:T(8,128)(2,1)S(1)}, u32[]{:S(2)}, u32[]{:S(2)}) %collective-permute-start.11) | collective-permute-done | bytes 65568 | tf_op jit(solution)/shard_map/ppermute | solution.py:19
  80.3 1.7 %collective-permute-start.16 = (bf16[512,512]{1,0:T(8,128)(2,1)}, bf16[512,512]{1,0:T(8,128)(2,1)}, u32[]{:S(2)}, u32[]{:S(2)}) collective-permute-start(bf16[512,512]{1,0:T(8,128)(2,1)} %collective-permute-done.5), channel_id=1, source_target_pairs={{0,64},{32,96},{64,0},{96,32},{128,192},{160,224},{192,128},{224,1... | collective-permute-start | bytes 1572872 | tf_op jit(solution)/shard_map/ppermute | solution.py:19
  82.4 1.2 collective-permute-done.12
  83.7 1.4 %top_cotangent.1.cot_ref.top_ref = bf16[256,1024]{1,0:T(8,128)(2,1)S(1)} custom-call(bf16[256,512]{1,0:T(8,128)(2,1)S(1)} %maximum_select_fusion.dlogits_ref, bf16[32,144,128]{2,1,0:T(8,128)(2,1)S(1)} %bitcast.49), custom_call_target="tpu_custom_call" | custom-call | tf_op jit(solution)/shard_map/top_cotangent/pallas_call | solution.py:130
  85.1 6.3 %upper.2 = bf16[256,512]{1,0:T(8,128)(2,1)} custom-call(s32[4]{0:T(128)S(1)} %pad_add_fusion.place_ref, bf16[256,1024]{1,0:T(8,128)(2,1)S(1)} %top_cotangent.1.cot_ref.top_ref, bf16[512,512]{1,0:T(8,128)(2,1)S(1)} %copy-done.5, bf16[512,512]{1,0:T(8,128)(2,1)} %collective-permute-done.13.side, bf16[512,512]{1,0:T(8,128)(2,1)} %collective-permute-done.8.over, ...), custom_call_target="tpu_custom_call" | custom-call | tf_op jit(solution)/shard_map/upper/pallas_call | solution.py:229
  91.4 1.3 collective-permute-start.14
  92.7 1.4 %all-to-all-done.1 = bf16[16,2,256,128]{3,2,1,0:T(8,128)(2,1)S(1)} async-done(((bf16[16,2,256,128]{3,2,1,0:T(8,128)(2,1)}), bf16[16,2,256,128]{3,2,1,0:T(8,128)(2,1)S(1)}, u32[]{:S(2)}, u32[]{:S(2)}) %all-to-all-start.1) | async-done | bytes 2097184 | tf_op jit(solution)/shard_map/all_to_all | solution.py:315
  94.1 2.2 %copy-done.2 = bf16[2,2,1,128,4096]{4,3,2,1,0:T(8,128)(2,1)S(1)} copy-done((bf16[2,2,1,128,4096]{4,3,2,1,0:T(8,128)(2,1)S(1)}, bf16[2,2,1,128,4096]{4,3,2,1,0:T(8,128)(2,1)}, u32[]{:S(2)}) %copy-start.2) | copy-done | bytes 4194328
  96.3 1.2 rows_in.1.refs_2_
  97.6 5.5 %upper.3 = bf16[256,512]{1,0:T(8,128)(2,1)S(1)} custom-call(s32[4]{0:T(128)S(1)} %pad_add_fusion.place_ref, bf16[256,1024]{1,0:T(8,128)(2,1)S(1)} %top_cotangent.1.cot_ref.top_ref, bf16[512,512]{1,0:T(8,128)(2,1)S(1)} %copy-done.4, bf16[512,512]{1,0:T(8,128)(2,1)} %collective-permute-done.15.side, bf16[512,512]{1,0:T(8,128)(2,1)S(1)} %copy-done.7, ...), custom_call_target="tpu_custom_call" | custom-call | tf_op jit(solution)/shard_map/upper/pallas_call | solution.py:229
  103.1 1.3 collective-permute-start.17
  104.4 4.2 %collective-permute-start.20 = (bf16[256,128]{1,0:T(8,128)(2,1)S(1)}, bf16[256,128]{1,0:T(8,128)(2,1)S(1)}, u32[]{:S(2)}, u32[]{:S(2)}) collective-permute-start(bf16[256,128]{1,0:T(8,128)(2,1)S(1)} %convert_element_type.29), channel_id=1, source_target_pairs={{0,96},{32,64},{64,32},{96,0},{128,224},{160,192},{192,160},{224,1... | collective-permute-start | bytes 196616 | tf_op jit(solution)/shard_map/ppermute | solution.py:19
  108.6 1.3 collective-permute-start.19
  109.9 5.6 %lower.2.refs_0_ = f32[4,256,128]{2,1,0:T(8,128)S(1)} custom-call(s32[4]{0:T(128)S(1)} %pad_add_fusion.place_ref, bf16[256,1024]{1,0:T(8,128)(2,1)S(1)} %top_cotangent.1.cot_ref.top_ref, bf16[256,512]{1,0:T(8,128)(2,1)} %collective-permute-done.14.recv_ref, bf16[512,512]{1,0:T(8,128)(2,1)S(1)} %copy-done.5, bf16[512,512]{1,0:T(8,128)(2,1)} %collective-permute-done.13.side, ...), custom_call_target="tpu_custom_call" | custom-call | tf_op jit(solution)/shard_map/lower/pallas_call | solution.py:240
  115.5 5.3 %collective-permute-done.17.recv_ref = bf16[256,512]{1,0:T(8,128)(2,1)S(1)} collective-permute-done((bf16[256,512]{1,0:T(8,128)(2,1)S(1)}, bf16[256,512]{1,0:T(8,128)(2,1)S(1)}, u32[]{:S(2)}, u32[]{:S(2)}) %collective-permute-start.17) | collective-permute-done | bytes 262176 | tf_op jit(solution)/shard_map/ppermute | solution.py:395
  120.8 5.4 %lower.3.refs_1_ = f32[4,256,128]{2,1,0:T(8,128)S(1)} custom-call(s32[4]{0:T(128)S(1)} %pad_add_fusion.place_ref, bf16[256,1024]{1,0:T(8,128)(2,1)S(1)} %top_cotangent.1.cot_ref.top_ref, bf16[256,512]{1,0:T(8,128)(2,1)S(1)} %collective-permute-done.17.recv_ref, bf16[512,512]{1,0:T(8,128)(2,1)S(1)} %copy-done.4, ...), custom_call_target="tpu_custom_call" | custom-call | tf_op jit(solution)/shard_map/lower/pallas_call | solution.py:240
  126.2 0.8 terms.1
  127.1 1.2 collective-permute-done.21
  128.3 0.7 collective-permute-start.23
  129.0 3.7 %collective-permute-start.22 = (f32[64,128]{1,0:T(8,128)S(1)}, f32[64,128]{1,0:T(8,128)S(1)}, u32[]{:S(2)}, u32[]{:S(2)}) collective-permute-start(f32[64,128]{1,0:T(8,128)S(1)} %add.191), channel_id=1, source_target_pairs={{0,64},{32,96},{64,0},{96,32},{128,192},{160,224},{192,128},{224,1... | collective-permute-start | bytes 98312 | tf_op jit(solution)/shard_map/ppermute | solution.py:19
  132.7 1.6 %collective-permute-done.24 = f32[64,128]{1,0:T(8,128)S(1)} collective-permute-done((f32[64,128]{1,0:T(8,128)S(1)}, f32[64,128]{1,0:T(8,128)S(1)}, u32[]{:S(2)}, u32[]{:S(2)}) %collective-permute-start.24) | collective-permute-done | bytes 32800 | tf_op jit(solution)/shard_map/ppermute | solution.py:19
  134.2 0.3 collective-permute-done.22
  134.7 0.7 reshape.81
  (93 shorter events, 2.3 us)
Async XLA Ops:
  1.1 6.4 %copy-start.13 = (bf16[2,8,128]{2,1,0:T(8,128)(2,1)S(1)}, bf16[2,8,128]{2,1,0:T(8,128)(2,1)}, u32[]{:S(2)}) copy-start(bf16[2,8,128]{2,1,0:T(8,128)(2,1)} %param.9) | copy-start | bytes 12292
  1.1 6.4 %copy-start.11 = (bf16[2,128,128]{2,1,0:T(8,128)(2,1)S(1)}, bf16[2,128,128]{2,1,0:T(8,128)(2,1)}, u32[]{:S(2)}) copy-start(bf16[2,128,128]{2,1,0:T(8,128)(2,1)} %param.10) | copy-start | bytes 196612
  1.1 6.7 %copy-start.12 = (bf16[128,512]{1,0:T(8,128)(2,1)S(1)}, bf16[128,512]{1,0:T(8,128)(2,1)}, u32[]{:S(2)}) copy-start(bf16[128,512]{1,0:T(8,128)(2,1)} %param.12) | copy-start | bytes 393220
  1.1 11.8 %copy-start.3 = (bf16[2,1,128,4096]{3,2,1,0:T(8,128)(2,1)S(1)}, bf16[2,1,128,4096]{3,2,1,0:T(8,128)(2,1)}, u32[]{:S(2)}) copy-start(bf16[2,1,128,4096]{3,2,1,0:T(8,128)(2,1)} %param.11) | copy-start | bytes 6291460
  6.8 24.2 %collective-permute-start.4 = (bf16[512,512]{1,0:T(8,128)(2,1)}, bf16[512,512]{1,0:T(8,128)(2,1)}, u32[]{:S(2)}, u32[]{:S(2)}) collective-permute-start(bf16[512,512]{1,0:T(8,128)(2,1)} %get-tuple-element.38), channel_id=1, source_target_pairs={{0,32},{32,0},{64,96},{96,64},{128,160},{160,128},{192,224},{224,1... | collective-permute-start | bytes 1572872 | tf_op jit(solution)/shard_map/ppermute | solution.py:19
  6.8 24.2 %collective-permute-start.5 = (bf16[512,512]{1,0:T(8,128)(2,1)}, bf16[512,512]{1,0:T(8,128)(2,1)}, u32[]{:S(2)}, u32[]{:S(2)}) collective-permute-start(bf16[512,512]{1,0:T(8,128)(2,1)} %get-tuple-element.39), channel_id=1, source_target_pairs={{0,32},{32,0},{64,96},{96,64},{128,160},{160,128},{192,224},{224,1... | collective-permute-start | bytes 1572872 | tf_op jit(solution)/shard_map/ppermute | solution.py:19
  7.3 23.7 %collective-permute-start.6 = (bf16[512,512]{1,0:T(8,128)(2,1)}, bf16[512,512]{1,0:T(8,128)(2,1)S(1)}, u32[]{:S(2)}, u32[]{:S(2)}) collective-permute-start(bf16[512,512]{1,0:T(8,128)(2,1)} %get-tuple-element.35), channel_id=1, source_target_pairs={{0,64},{32,96},{64,0},{96,32},{128,192},{160,224},{192,128},{224,1... | collective-permute-start | bytes 1572872 | tf_op jit(solution)/shard_map/ppermute | solution.py:19
  7.7 6.8 %collective-permute-start.1 = (bf16[2,36,128]{2,1,0:T(8,128)(2,1)S(1)}, bf16[2,36,128]{2,1,0:T(8,128)(2,1)S(1)}, u32[]{:S(2)}, u32[]{:S(2)}) collective-permute-start(bf16[2,36,128]{2,1,0:T(8,128)(2,1)S(1)} %get-tuple-element.69), channel_id=1, source_target_pairs={{0,32},{32,0},{64,96},{96,64},{128,160},{160,128},{192,224},{224,1... | collective-permute-start | bytes 55304 | tf_op jit(solution)/shard_map/ppermute | solution.py:19
  7.9 8.6 %collective-permute-start = (bf16[128,128]{1,0:T(8,128)(2,1)S(1)}, bf16[128,128]{1,0:T(8,128)(2,1)S(1)}, u32[]{:S(2)}, u32[]{:S(2)}) collective-permute-start(bf16[128,128]{1,0:T(8,128)(2,1)S(1)} %bitcast.69), channel_id=1, source_target_pairs={{0,208},{1,209},{2,210},{3,211},{4,212},{5,213},{6,214},{7,215},{8... | collective-permute-start | bytes 98312 | tf_op jit(solution)/shard_map/ppermute | solution.py:341
  13.6 0.8 copy-start.8
  14.5 8.1 %collective-permute-start.2 = (bf16[2,36,128]{2,1,0:T(8,128)(2,1)S(1)}, bf16[2,36,128]{2,1,0:T(8,128)(2,1)S(1)}, u32[]{:S(2)}, u32[]{:S(2)}) collective-permute-start(bf16[2,36,128]{2,1,0:T(8,128)(2,1)S(1)} %get-tuple-element.68), channel_id=1, source_target_pairs={{0,64},{32,96},{64,0},{96,32},{128,192},{160,224},{192,128},{224,1... | collective-permute-start | bytes 55304 | tf_op jit(solution)/shard_map/ppermute | solution.py:19
  22.7 33.3 %copy-start.9 = (bf16[256,1024]{1,0:T(8,128)(2,1)S(1)}, bf16[256,1024]{1,0:T(8,128)(2,1)}, u32[]{:S(2)}) copy-start(bf16[256,1024]{1,0:T(8,128)(2,1)} %copy-done.8) | copy-start | bytes 1572868
  22.7 8.3 %collective-permute-start.3 = (bf16[272,128]{1,0:T(8,128)(2,1)S(1)}, bf16[272,128]{1,0:T(8,128)(2,1)S(1)}, u32[]{:S(2)}, u32[]{:S(2)}) collective-permute-start(bf16[272,128]{1,0:T(8,128)(2,1)S(1)} %pad_maximum_fusion.2), channel_id=1, source_target_pairs={{0,16},{1,17},{2,18},{3,19},{4,20},{5,21},{6,22},{7,23},{8,24},{9,... | collective-permute-start | bytes 208904 | tf_op jit(solution)/shard_map/ppermute | solution.py:19
  31.0 1.3 copy-start.6
  32.3 23.7 %all-to-all-start = ((bf16[16,2,144,128]{3,2,1,0:T(8,128)(2,1)}), bf16[16,2,144,128]{3,2,1,0:T(8,128)(2,1)S(1)}, u32[]{:S(2)}, u32[]{:S(2)}) async-start(bf16[16,2,144,128]{3,2,1,0:T(8,128)(2,1)} %broadcast_in_dim.4), calls=%async_computation | async-start | bytes 2359296 | tf_op jit(solution)/shard_map/all_to_all | solution.py:315
  38.9 25.5 %collective-permute-start.8 = (bf16[512,512]{1,0:T(8,128)(2,1)}, bf16[512,512]{1,0:T(8,128)(2,1)}, u32[]{:S(2)}, u32[]{:S(2)}) collective-permute-start(bf16[512,512]{1,0:T(8,128)(2,1)} %get-tuple-element.48), channel_id=1, source_target_pairs={{0,64},{32,96},{64,0},{96,32},{128,192},{160,224},{192,128},{224,1... | collective-permute-start | bytes 1572872 | tf_op jit(solution)/shard_map/ppermute | solution.py:19
  44.3 21.7 %collective-permute-start.9 = (bf16[512,512]{1,0:T(8,128)(2,1)}, bf16[512,512]{1,0:T(8,128)(2,1)}, u32[]{:S(2)}, u32[]{:S(2)}) collective-permute-start(bf16[512,512]{1,0:T(8,128)(2,1)} %collective-permute-done.4), channel_id=1, source_target_pairs={{0,64},{32,96},{64,0},{96,32},{128,192},{160,224},{192,128},{224,1... | collective-permute-start | bytes 1572872 | tf_op jit(solution)/shard_map/ppermute | solution.py:19
  55.9 21.9 %copy-start = (bf16[16,2,144,128]{3,2,1,0:T(8,128)(2,1)}, bf16[16,2,144,128]{3,2,1,0:T(8,128)(2,1)S(1)}, u32[]{:S(2)}) copy-start(bf16[16,2,144,128]{3,2,1,0:T(8,128)(2,1)S(1)} %all-to-all-done) | copy-start | bytes 3538948
  57.7 5.7 %collective-permute-start.7 = (f32[128,512]{1,0:T(8,128)}, f32[128,512]{1,0:T(8,128)}, u32[]{:S(2)}, u32[]{:S(2)}) collective-permute-start(f32[128,512]{1,0:T(8,128)} %get-tuple-element.47), channel_id=1, source_target_pairs={{0,32},{32,0},{64,96},{96,64},{128,160},{160,128},{192,224},{224,1... | collective-permute-start | bytes 786440 | tf_op jit(solution)/shard_map/ppermute | solution.py:19
  59.5 11.5 %copy-start.14 = (s32[2,1,128]{2,1,0:T(1,128)S(1)}, s32[2,1,128]{2,1,0:T(1,128)}, u32[]{:S(2)}) copy-start(s32[2,1,128]{2,1,0:T(1,128)} %param.13) | copy-start | bytes 3076
  59.5 34.6 %all-to-all-start.1 = ((bf16[16,2,256,128]{3,2,1,0:T(8,128)(2,1)}), bf16[16,2,256,128]{3,2,1,0:T(8,128)(2,1)S(1)}, u32[]{:S(2)}, u32[]{:S(2)}) async-start(bf16[16,2,256,128]{3,2,1,0:T(8,128)(2,1)} %broadcast_in_dim.5), calls=%async_computation.1 | async-start | bytes 4194304 | tf_op jit(solution)/shard_map/all_to_all | solution.py:315
  64.4 1.6 %copy-start.10 = (f32[128,512]{1,0:T(8,128)}, f32[128,512]{1,0:T(8,128)S(1)}, u32[]{:S(2)}) copy-start(f32[128,512]{1,0:T(8,128)S(1)} %add.185) | copy-start | bytes 786436
  66.0 8.6 %collective-permute-start.10 = (f32[64,512]{1,0:T(8,128)S(1)}, f32[64,512]{1,0:T(8,128)S(1)}, u32[]{:S(2)}, u32[]{:S(2)}) collective-permute-start(f32[64,512]{1,0:T(8,128)S(1)} %constant_dynamic-slice_fusion), channel_id=1, source_target_pairs={{0,64},{32,96},{64,0},{96,32},{128,192},{160,224},{192,128},{224,1... | collective-permute-start | bytes 393224 | tf_op jit(solution)/shard_map/ppermute | solution.py:19
  70.5 14.7 %collective-permute-start.13 = (bf16[512,512]{1,0:T(8,128)(2,1)}, bf16[512,512]{1,0:T(8,128)(2,1)}, u32[]{:S(2)}, u32[]{:S(2)}) collective-permute-start(bf16[512,512]{1,0:T(8,128)(2,1)} %get-tuple-element.36), channel_id=1, source_target_pairs={{0,32},{32,0},{64,96},{96,64},{128,160},{160,128},{192,224},{224,1... | collective-permute-start | bytes 1572872 | tf_op jit(solution)/shard_map/ppermute | solution.py:19
  70.7 26.8 %collective-permute-start.15 = (bf16[512,512]{1,0:T(8,128)(2,1)}, bf16[512,512]{1,0:T(8,128)(2,1)}, u32[]{:S(2)}, u32[]{:S(2)}) collective-permute-start(bf16[512,512]{1,0:T(8,128)(2,1)} %get-tuple-element.37), channel_id=1, source_target_pairs={{0,32},{32,0},{64,96},{96,64},{128,160},{160,128},{192,224},{224,1... | collective-permute-start | bytes 1572872 | tf_op jit(solution)/shard_map/ppermute | solution.py:19
  76.0 4.4 %collective-permute-start.11 = (bf16[64,512]{1,0:T(8,128)(2,1)S(1)}, bf16[64,512]{1,0:T(8,128)(2,1)S(1)}, u32[]{:S(2)}, u32[]{:S(2)}) collective-permute-start(bf16[64,512]{1,0:T(8,128)(2,1)S(1)} %subtract_convert_fusion), channel_id=1, source_target_pairs={{0,64},{32,96},{64,0},{96,32},{128,192},{160,224},{192,128},{224,1... | collective-permute-start | bytes 196616 | tf_op jit(solution)/shard_map/ppermute | solution.py:19
  77.8 5.9 %copy-start.1 = (bf16[16,2,144,128]{3,2,1,0:T(8,128)(2,1)S(1)}, bf16[16,2,144,128]{3,2,1,0:T(8,128)(2,1)}, u32[]{:S(2)}) copy-start(bf16[16,2,144,128]{3,2,1,0:T(8,128)(2,1)} %copy-done) | copy-start | bytes 3538948
  77.9 7.3 %copy-start.5 = (bf16[512,512]{1,0:T(8,128)(2,1)S(1)}, bf16[512,512]{1,0:T(8,128)(2,1)}, u32[]{:S(2)}) copy-start(bf16[512,512]{1,0:T(8,128)(2,1)} %get-tuple-element.32.near) | copy-start | bytes 1572868
  80.3 17.2 %collective-permute-start.16 = (bf16[512,512]{1,0:T(8,128)(2,1)}, bf16[512,512]{1,0:T(8,128)(2,1)}, u32[]{:S(2)}, u32[]{:S(2)}) collective-permute-start(bf16[512,512]{1,0:T(8,128)(2,1)} %collective-permute-done.5), channel_id=1, source_target_pairs={{0,64},{32,96},{64,0},{96,32},{128,192},{160,224},{192,128},{224,1... | collective-permute-start | bytes 1572872 | tf_op jit(solution)/shard_map/ppermute | solution.py:19
  82.2 1.4 %collective-permute-start.12 = (bf16[128,512]{1,0:T(8,128)(2,1)S(1)}, bf16[128,512]{1,0:T(8,128)(2,1)S(1)}, u32[]{:S(2)}, u32[]{:S(2)}) collective-permute-start(bf16[128,512]{1,0:T(8,128)(2,1)S(1)} %maximum_select_fusion.2), channel_id=1, source_target_pairs={{0,32},{32,0},{64,96},{96,64},{128,160},{160,128},{192,224},{224,1... | collective-permute-start | bytes 393224 | tf_op jit(solution)/shard_map/ppermute | solution.py:19
  91.4 18.4 %collective-permute-start.14 = (bf16[256,512]{1,0:T(8,128)(2,1)}, bf16[256,512]{1,0:T(8,128)(2,1)}, u32[]{:S(2)}, u32[]{:S(2)}) collective-permute-start(bf16[256,512]{1,0:T(8,128)(2,1)} %upper.2), channel_id=1, source_target_pairs={{128,0},{160,32},{192,64},{224,96},{129,1},{161,33},{193,65},{225,... | collective-permute-start | bytes 786440 | tf_op jit(solution)/shard_map/ppermute | solution.py:392
  94.1 2.2 %copy-start.2 = (bf16[2,2,1,128,4096]{4,3,2,1,0:T(8,128)(2,1)S(1)}, bf16[2,2,1,128,4096]{4,3,2,1,0:T(8,128)(2,1)}, u32[]{:S(2)}) copy-start(bf16[2,2,1,128,4096]{4,3,2,1,0:T(8,128)(2,1)} %param.7) | copy-start | bytes 12582916
  96.3 1.3 copy-start.4
  96.3 1.3 copy-start.7
  103.1 17.7 %collective-permute-start.17 = (bf16[256,512]{1,0:T(8,128)(2,1)S(1)}, bf16[256,512]{1,0:T(8,128)(2,1)S(1)}, u32[]{:S(2)}, u32[]{:S(2)}) collective-permute-start(bf16[256,512]{1,0:T(8,128)(2,1)S(1)} %upper.3), channel_id=1, source_target_pairs={{128,0},{160,32},{192,64},{224,96},{129,1},{161,33},{193,65},{225,... | collective-permute-start | bytes 786440 | tf_op jit(solution)/shard_map/ppermute | solution.py:395
  104.4 21.8 %collective-permute-start.20 = (bf16[256,128]{1,0:T(8,128)(2,1)S(1)}, bf16[256,128]{1,0:T(8,128)(2,1)S(1)}, u32[]{:S(2)}, u32[]{:S(2)}) collective-permute-start(bf16[256,128]{1,0:T(8,128)(2,1)S(1)} %convert_element_type.29), channel_id=1, source_target_pairs={{0,96},{32,64},{64,32},{96,0},{128,224},{160,192},{192,160},{224,1... | collective-permute-start | bytes 196616 | tf_op jit(solution)/shard_map/ppermute | solution.py:19
  108.6 17.6 %collective-permute-start.19 = (bf16[256,128]{1,0:T(8,128)(2,1)S(1)}, bf16[256,128]{1,0:T(8,128)(2,1)S(1)}, u32[]{:S(2)}, u32[]{:S(2)}) collective-permute-start(bf16[256,128]{1,0:T(8,128)(2,1)S(1)} %convert_element_type.29), channel_id=1, source_target_pairs={{0,64},{32,96},{64,0},{96,32},{128,192},{160,224},{192,128},{224,1... | collective-permute-start | bytes 196616 | tf_op jit(solution)/shard_map/ppermute | solution.py:19
  109.8 16.4 %collective-permute-start.18 = (bf16[256,128]{1,0:T(8,128)(2,1)S(1)}, bf16[256,128]{1,0:T(8,128)(2,1)S(1)}, u32[]{:S(2)}, u32[]{:S(2)}) collective-permute-start(bf16[256,128]{1,0:T(8,128)(2,1)S(1)} %convert_element_type.29), channel_id=1, source_target_pairs={{0,32},{32,0},{64,96},{96,64},{128,160},{160,128},{192,224},{224,1... | collective-permute-start | bytes 196616 | tf_op jit(solution)/shard_map/ppermute | solution.py:19
  127.0 1.2 collective-permute-start.21
  128.3 6.0 %collective-permute-start.24 = (f32[64,128]{1,0:T(8,128)S(1)}, f32[64,128]{1,0:T(8,128)S(1)}, u32[]{:S(2)}, u32[]{:S(2)}) collective-permute-start(f32[64,128]{1,0:T(8,128)S(1)} %add.191), channel_id=1, source_target_pairs={{0,192},{32,224},{64,128},{96,160},{128,64},{160,96},{192,0},{224,... | collective-permute-start | bytes 98312 | tf_op jit(solution)/shard_map/ppermute | solution.py:19
  128.3 6.0 %collective-permute-start.23 = (f32[64,128]{1,0:T(8,128)S(1)}, f32[64,128]{1,0:T(8,128)S(1)}, u32[]{:S(2)}, u32[]{:S(2)}) collective-permute-start(f32[64,128]{1,0:T(8,128)S(1)} %add.191), channel_id=1, source_target_pairs={{0,128},{32,160},{64,192},{96,224},{128,0},{160,32},{192,64},{224,... | collective-permute-start | bytes 98312 | tf_op jit(solution)/shard_map/ppermute | solution.py:19
  129.0 5.6 %collective-permute-start.22 = (f32[64,128]{1,0:T(8,128)S(1)}, f32[64,128]{1,0:T(8,128)S(1)}, u32[]{:S(2)}, u32[]{:S(2)}) collective-permute-start(f32[64,128]{1,0:T(8,128)S(1)} %add.191), channel_id=1, source_target_pairs={{0,64},{32,96},{64,0},{96,32},{128,192},{160,224},{192,128},{224,1... | collective-permute-start | bytes 98312 | tf_op jit(solution)/shard_map/ppermute | solution.py:19
